TPU v7x, 256 devices: a whole 4x4x8 slice. The times are simulated.
256 devices in a mesh: atm: 32 (over z, y_hi, core), ocn: 8 (over x, y_lo).
Axes of the slice: x: 4, y: 4 (y_hi: 2, y_lo: 2; y = y_hi * 2 + y_lo), z: 8, core: 2. Of those that a mesh axis runs over, the one named last changes fastest.
Arguments:
- atm_state: float32 [7, 72, 128, 512], P(None, 'ocn', 'atm'), may hold values from -6 to 6
- level_diffusion: float32 [72], P('ocn'), may hold values from 0.05 to 0.2
- level_wind: float32 [72], P('ocn'), may hold values from -0.2 to 0.2
- vertical_rate: float32 [7], replicated, may hold values from 0.05 to 0.2
- convective_rate: float32 [7], replicated, may hold values from 0.05 to 0.4
- ocean_skin: float32 [65536], P(('atm', 'ocn')), may hold values from -6 to 6
- trigger: int32 [65536], P(('atm', 'ocn')), may hold values from 0 to 1, as said below
- group_order: int32 [65536], P(('atm', 'ocn')), may hold values from 0 to 255, as said below
- ocean_state: float32 [2, 20, 262144], P(None, None, ('atm', 'ocn')), may hold values from -6 to 6
- ocean_neighbors: int32 [6, 262144], P(None, ('atm', 'ocn')), may hold values from -32 to 32, as said below
- flux_sources: int32 [4, 262144], P(None, ('atm', 'ocn')), may hold values from 0 to 65535, as said below
- flux_weights: float32 [4, 262144], P(None, ('atm', 'ocn')), may hold values from 0.1 to 0.5
- surface_sources: int32 [4, 65536], P(None, ('atm', 'ocn')), may hold values from 0 to 262143, as said below
- surface_weights: float32 [4, 65536], P(None, ('atm', 'ocn')), may hold values from 0.1 to 0.5
Outputs:
- atm_new: float32 [7, 72, 128, 512], P(None, 'ocn', 'atm')
- ocean_new: float32 [2, 20, 262144], P(None, None, ('atm', 'ocn'))
- surface_new: float32 [65536], P(('atm', 'ocn'))
Inputs may be any that keep to these rules, and one draw needn't show every extreme that they name: `group_order`: within each block of 256 entries the values are a permutation of 0 to 255. `trigger`: every aligned run of 8 entries holds equally many ones within a block of 256, so each physics group (run k of every device of an ocn index) holds exactly 64 ones. One block of 256 holds at most 160 ones, and some block holds exactly that many. `ocean_neighbors`: cell plus offset is always a cell of the grid. `flux_sources`: the sources of cell c lie within 8 columns of c // 4. `surface_sources`: the sources of column k lie within 32 cells of 4 * k.
All inputs are finite; a program needn't handle non-finite values.
Results may differ from a plain program's by a relative error of at most 0.00007.
Values sent between devices are 32-bit elements; how exact they have to be, the bound alone decides.
A program may use at most 64 MiB of HBM per device.

v0:
```python
import jax
import jax.numpy as jnp
from jax import lax
from jax.sharding import PartitionSpec as P

DYN_STEPS = 4
PHYS_ITERS = 3
CONV_ITERS = 24
NBR = 6
NW = 4
HW = 32
RW = 8
RW2 = 32
OSTEPS = 4


OCEAN_SPREAD = 0.6
OCEAN_VERTICAL = 0.2
HEAT_COEF = 0.5
MOIST_COEF = 0.5
HEAT_BACK = 0.3
MOIST_BACK = 0.3
OCEAN_FORCE = 0.3


def extended_2(block, sides, width):
    for axis, dim in sides:
        count = lax.axis_size(axis)
        forward = [(i, i + 1) for i in range(count - 1)]
        backward = [(target, source) for source, target in forward]
        low = lax.ppermute(
            lax.slice_in_dim(block, block.shape[dim] - width, None, axis=dim), axis, forward
        )
        high = lax.ppermute(lax.slice_in_dim(block, 0, width, axis=dim), axis, backward)
        block = jnp.concatenate([low, block, high], axis=dim)
    return block


def grid_step(prognostic, padded, level_diffusion, level_wind):
    northern = padded[:, :, :-2]
    southern = padded[:, :, 2:]
    eastern = jnp.roll(prognostic, -1, axis=3)
    western = jnp.roll(prognostic, 1, axis=3)
    laplace = northern + southern + eastern + western - 4.0 * prognostic
    return (
        prognostic
        + level_diffusion[None, :, None, None] * laplace
        - level_wind[None, :, None, None] * 0.5 * (eastern - western)
    )


def vertical(columns, vertical_rate):
    for repeat in range(PHYS_ITERS):
        padded = jnp.concatenate([columns[:, :1], columns, columns[:, -1:]], axis=1)
        columns = columns + vertical_rate[:, None, None] * (
            padded[:, 2:] + padded[:, :-2] - 2.0 * columns
        )
    return columns


def convect(columns, convective_rate, trigger_mask):
    for repeat in range(CONV_ITERS):
        transfer = (
            convective_rate[:, None, None]
            * jnp.tanh(columns[:, 1:] - columns[:, :-1])
            * trigger_mask
        )
        columns = (
            columns
            + jnp.pad(transfer, ((0, 0), (0, 1), (0, 0)))
            - jnp.pad(transfer, ((0, 0), (1, 0), (0, 0)))
        )
    return columns


def convect_picked(columns, convective_rate, mask_row, count):
    total = columns.shape[2]
    picked = jnp.nonzero(mask_row > 0.5, size=count, fill_value=total)[0]
    chosen = jnp.take(columns, picked, axis=2, mode="fill", fill_value=0.0)
    chosen = convect(chosen, convective_rate, 1.0)
    return columns.at[:, :, picked].set(chosen, mode="drop")


def surface(columns, skin_value):
    lowest = columns[:, -1, :]
    wind_speed = jnp.sqrt(1.0 + lowest[1] * lowest[1] + lowest[2] * lowest[2])
    heat_flux = HEAT_COEF * wind_speed * (lowest[0] - skin_value)
    fresh_flux = MOIST_COEF * wind_speed * lowest[3]
    columns = columns.at[0, -1].add(-HEAT_BACK * heat_flux)
    columns = columns.at[3, -1].add(-MOIST_BACK * fresh_flux)
    return (columns, jnp.stack([heat_flux, fresh_flux]))


def ocean_update(ocean_fields, beside_all, forcing):
    blended = ocean_fields + OCEAN_SPREAD * (beside_all / 6.0 - ocean_fields)
    padded = jnp.concatenate([blended[:, :1], blended, blended[:, -1:]], axis=1)
    blended = blended + OCEAN_VERTICAL * (padded[:, 2:] + padded[:, :-2] - 2.0 * blended)
    return blended.at[:, 0].add(OCEAN_FORCE * forcing)


def local(
    atm_state,
    level_diffusion,
    level_wind,
    vertical_rate,
    convective_rate,
    ocean_skin,
    trigger,
    group_order,
    ocean_state,
    ocean_neighbors,
    flux_sources,
    flux_weights,
    surface_sources,
    surface_weights,
):
    fields, levels_here, block_rows, longitudes = atm_state.shape
    prognostic = atm_state
    for repeat in range(DYN_STEPS):
        padded = extended_2(prognostic, (("atm", 2),), 1)
        prognostic = grid_step(prognostic, padded, level_diffusion, level_wind)
    columns = prognostic.reshape(fields, levels_here, block_rows * longitudes)
    columns = lax.all_to_all(columns, "ocn", split_axis=2, concat_axis=1, tiled=True)
    columns = vertical(columns, vertical_rate)
    active = jnp.zeros(group_order.shape, jnp.int32).at[group_order].set(trigger)
    columns = convect_picked(
        columns, convective_rate, active.astype(jnp.float32), columns.shape[2] * 5 // 8
    )
    columns, fluxes = surface(columns, ocean_skin)
    columns = lax.all_to_all(columns, "ocn", split_axis=1, concat_axis=2, tiled=True)
    atm_new = columns.reshape(fields, levels_here, block_rows, longitudes)
    column_count = fluxes.shape[1]
    cell_count = ocean_state.shape[2]
    offset = lax.axis_index(("atm", "ocn"))
    nearby = extended_2(fluxes, ((("atm", "ocn"), 1),), RW)
    indices = flux_sources - (offset * column_count - RW)
    forcing = jnp.zeros((2, cell_count), jnp.float32)
    for link in range(NW):
        forcing = forcing + flux_weights[link][None, :] * jnp.take(nearby, indices[link], axis=1)
    ocean_fields = ocean_state
    neighbor_index = ocean_neighbors + HW + jnp.arange(cell_count, dtype=jnp.int32)[None, :]
    for repeat in range(OSTEPS):
        extended = extended_2(ocean_fields, ((("atm", "ocn"), 2),), HW)
        beside_all = jnp.zeros_like(ocean_fields)
        for link in range(NBR):
            beside_all = beside_all + jnp.take(extended, neighbor_index[link], axis=2)
        ocean_fields = ocean_update(ocean_fields, beside_all, forcing)
    uppermost = extended_2(ocean_fields[0, 0], ((("atm", "ocn"), 0),), RW2)
    surface_index = surface_sources - (offset * cell_count - RW2)
    surface_new = jnp.zeros((column_count,), jnp.float32)
    for link in range(NW):
        surface_new = surface_new + surface_weights[link] * jnp.take(uppermost, surface_index[link])
    return (atm_new, ocean_fields, surface_new)


def solution(mesh):
    return jax.shard_map(
        local,
        mesh=mesh,
        in_specs=(
            P(None, "ocn", "atm", None),
            P("ocn"),
            P("ocn"),
            P(),
            P(),
            P(("atm", "ocn")),
            P(("atm", "ocn")),
            P(("atm", "ocn")),
            P(None, None, ("atm", "ocn")),
            P(None, ("atm", "ocn")),
            P(None, ("atm", "ocn")),
            P(None, ("atm", "ocn")),
            P(None, ("atm", "ocn")),
            P(None, ("atm", "ocn")),
        ),
        out_specs=(P(None, "ocn", "atm", None), P(None, None, ("atm", "ocn")), P(("atm", "ocn"))),
        check_vma=False,
    )
```

profile of v0, /device:TPU:127, one launch (start us, length us, event | category | flops | bytes accessed | tf_op | source)
XLA Modules:
  0.0 505.9 jit_solution(16055800237237025156)
XLA Ops:
  38.8 7.5 %gather_fusion.1 = f32[1024,2,20]{2,1,0:T(2,128)} fusion(f32[2,20,1088]{1,0,2:T(2,128)S(1)} %copy.389, s32[1024]{0:T(1024)S(1)} %fusion.129), kind=kCustom, calls=%fused_computation.clone | custom fusion | bytes 331776 | tf_op jit(solution)/shard_map/jit(_take)/gather | solution.py:146
  47.8 7.5 %gather_fusion.2 = f32[1024,2,20]{2,1,0:T(2,128)} fusion(f32[2,20,1088]{1,0,2:T(2,128)S(1)} %copy.389, s32[1024]{0:T(1024)S(1)} %fusion.130), kind=kCustom, calls=%fused_computation.3.clone | custom fusion | bytes 331776 | tf_op jit(solution)/shard_map/jit(_take)/gather | solution.py:146
  56.8 7.5 %gather_fusion.3 = f32[1024,2,20]{2,1,0:T(2,128)} fusion(f32[2,20,1088]{1,0,2:T(2,128)S(1)} %copy.389, s32[1024]{0:T(1024)S(1)} %fusion.131), kind=kCustom, calls=%fused_computation.4.clone | custom fusion | bytes 331776 | tf_op jit(solution)/shard_map/jit(_take)/gather | solution.py:146
  65.8 7.5 %gather_fusion.4 = f32[1024,2,20]{2,1,0:T(2,128)} fusion(f32[2,20,1088]{1,0,2:T(2,128)S(1)} %copy.389, s32[1024]{0:T(1024)S(1)} %fusion.132), kind=kCustom, calls=%fused_computation.5.clone | custom fusion | bytes 331776 | tf_op jit(solution)/shard_map/jit(_take)/gather | solution.py:146
  74.8 7.5 %gather_fusion.5 = f32[1024,2,20]{2,1,0:T(2,128)} fusion(f32[2,20,1088]{1,0,2:T(2,128)S(1)} %copy.389, s32[1024]{0:T(1024)S(1)} %fusion.133), kind=kCustom, calls=%fused_computation.6.clone | custom fusion | bytes 331776 | tf_op jit(solution)/shard_map/jit(_take)/gather | solution.py:146
  84.4 7.5 %gather_fusion.6 = f32[1024,2,20]{2,1,0:T(2,128)} fusion(f32[2,20,1088]{1,0,2:T(2,128)S(1)} %copy.389, s32[1024]{0:T(1024)S(1)} %fusion.134), kind=kCustom, calls=%fused_computation.7.clone | custom fusion | bytes 331776 | tf_op jit(solution)/shard_map/jit(_take)/gather | solution.py:146
  103.6 7.8 %collective-permute-done.3 = f32[7,9,1,512]{3,2,1,0:T(1,128)S(1)} collective-permute-done((f32[7,9,1,512]{3,2,1,0:T(1,128)S(1)}, f32[7,9,1,512]{3,2,1,0:T(1,128)S(1)}, u32[]{:S(2)}, u32[]{:S(2)}) %collective-permute-start.3) | collective-permute-done | bytes 129056 | tf_op jit(solution)/shard_map/ppermute | solution.py:34
  150.9 8.1 %all-to-all-start = ((f32[8,1,16128]{2,1,0:T(1,128)}), f32[8,1,16128]{2,1,0:T(1,128)S(1)}, u32[]{:S(2)}, u32[]{:S(2)}) async-start(f32[8,1,16128]{2,1,0:T(1,128)} %reshape.741), calls=%async_computation | async-start | bytes 1032192 | tf_op jit(solution)/shard_map/all_to_all | solution.py:123
  211.7 8.4 %collective-permute-done.11 = f32[2,8]{1,0:T(2,128)S(1)} collective-permute-done((f32[2,8]{1,0:T(2,128)S(1)}, f32[2,8]{1,0:T(2,128)S(1)}, u32[]{:S(2)}, u32[]{:S(2)}) %collective-permute-start.11) | collective-permute-done | bytes 96 | tf_op jit(solution)/shard_map/ppermute | solution.py:34
  254.2 7.6 %gather_fusion.12 = f32[1024,2,20]{2,1,0:T(2,128)} fusion(f32[2,20,1088]{1,0,2:T(2,128)S(1)} %copy.409, s32[1024]{0:T(1024)S(1)} %fusion.130), kind=kCustom, calls=%fused_computation.9.clone | custom fusion | bytes 331776 | tf_op jit(solution)/shard_map/jit(_take)/gather | solution.py:146
  261.8 7.5 %gather_fusion.13 = f32[1024,2,20]{2,1,0:T(2,128)} fusion(f32[2,20,1088]{1,0,2:T(2,128)S(1)} %copy.409, s32[1024]{0:T(1024)S(1)} %fusion.131), kind=kCustom, calls=%fused_computation.10.clone | custom fusion | bytes 331776 | tf_op jit(solution)/shard_map/jit(_take)/gather | solution.py:146
  276.9 7.5 %gather_fusion.15 = f32[1024,2,20]{2,1,0:T(2,128)} fusion(f32[2,20,1088]{1,0,2:T(2,128)S(1)} %copy.409, s32[1024]{0:T(1024)S(1)} %fusion.133), kind=kCustom, calls=%fused_computation.12.clone | custom fusion | bytes 331776 | tf_op jit(solution)/shard_map/jit(_take)/gather | solution.py:146
  305.7 23.1 %scatter-add.29 = f32[7,72,256]{1,0,2:T(8,128)S(1)} dynamic-update-slice(f32[7,72,256]{1,0,2:T(8,128)S(1)} %copy.451, f32[1,1,256]{1,0,2:T(1,128)S(1)} %broadcast_select_fusion, s32[]{:T(128)} %bitcast.11, s32[]{:T(128)} %bitcast.12, s32[]{:T(128)} %constant.251.clone.1) | dynamic-update-slice | bytes 2052 | tf_op jit(solution)/shard_map/scatter-add | solution.py:89
  339.4 7.6 %gather_fusion.18 = f32[1024,2,20]{2,1,0:T(2,128)} fusion(f32[2,20,1088]{1,0,2:T(2,128)S(1)} %copy.421, s32[1024]{0:T(1024)S(1)} %copy-done.31), kind=kCustom, calls=%fused_computation.15.clone | custom fusion | bytes 331776 | tf_op jit(solution)/shard_map/jit(_take)/gather | solution.py:146
  354.6 7.5 %gather_fusion.20 = f32[1024,2,20]{2,1,0:T(2,128)} fusion(f32[2,20,1088]{1,0,2:T(2,128)S(1)} %copy.421, s32[1024]{0:T(1024)S(1)} %copy-done.25), kind=kCustom, calls=%fused_computation.17.clone | custom fusion | bytes 331776 | tf_op jit(solution)/shard_map/jit(_take)/gather | solution.py:146
  369.6 7.5 %gather_fusion.22 = f32[1024,2,20]{2,1,0:T(2,128)} fusion(f32[2,20,1088]{1,0,2:T(2,128)S(1)} %copy.421, s32[1024]{0:T(1024)S(1)} %fusion.134), kind=kCustom, calls=%fused_computation.19.clone | custom fusion | bytes 331776 | tf_op jit(solution)/shard_map/jit(_take)/gather | solution.py:146
  389.2 7.6 %collective-permute-start.16 = (f32[2,20,32]{2,0,1:T(2,128)S(1)}, f32[2,20,32]{2,0,1:T(2,128)S(1)}, u32[]{:S(2)}, u32[]{:S(2)}) collective-permute-start(f32[2,20,32]{2,0,1:T(2,128)S(1)} %get-tuple-element.144), channel_id=1, source_target_pairs={{0,1},{1,2},{2,3},{3,4},{4,5},{5,6},{6,7},{7,8},{8,9},{9,10},{10,1... | collective-permute-start | bytes 15368 | tf_op jit(solution)/shard_map/ppermute | solution.py:31
  399.4 21.8 %scatter-add.30 = f32[7,72,256]{1,0,2:T(8,128)S(1)} dynamic-update-slice(f32[7,72,256]{1,0,2:T(8,128)S(1)} %scatter-add.29, f32[1,1,256]{1,0,2:T(1,128)S(1)} %slice_add_fusion, s32[]{:T(128)} %constant.263.clone.1, s32[]{:T(128)} %constant.257.clone.1, s32[]{:T(128)} %constant.251.clone.1) | dynamic-update-slice | bytes 2052 | tf_op jit(solution)/shard_map/scatter-add | solution.py:90
  432.4 7.5 %gather_fusion.24 = f32[1024,2,20]{2,1,0:T(2,128)} fusion(f32[2,20,1088]{1,0,2:T(2,128)S(1)} %copy.433, s32[1024]{0:T(1024)S(1)} %copy-done.31), kind=kCustom, calls=%fused_computation.21.clone | custom fusion | bytes 331776 | tf_op jit(solution)/shard_map/jit(_take)/gather | solution.py:146
  439.9 7.6 %gather_fusion.25 = f32[1024,2,20]{2,1,0:T(2,128)} fusion(f32[2,20,1088]{1,0,2:T(2,128)S(1)} %copy.433, s32[1024]{0:T(1024)S(1)} %copy-done.27), kind=kCustom, calls=%fused_computation.22.clone | custom fusion | bytes 331776 | tf_op jit(solution)/shard_map/jit(_take)/gather | solution.py:146
  447.6 7.5 %gather_fusion.26 = f32[1024,2,20]{2,1,0:T(2,128)} fusion(f32[2,20,1088]{1,0,2:T(2,128)S(1)} %copy.433, s32[1024]{0:T(1024)S(1)} %copy-done.25), kind=kCustom, calls=%fused_computation.23.clone | custom fusion | bytes 331776 | tf_op jit(solution)/shard_map/jit(_take)/gather | solution.py:146
  462.6 7.5 %gather_fusion.28 = f32[1024,2,20]{2,1,0:T(2,128)} fusion(f32[2,20,1088]{1,0,2:T(2,128)S(1)} %copy.433, s32[1024]{0:T(1024)S(1)} %fusion.134), kind=kCustom, calls=%fused_computation.25.clone | custom fusion | bytes 331776 | tf_op jit(solution)/shard_map/jit(_take)/gather | solution.py:146
  478.0 7.8 %collective-permute-start.18 = (f32[32]{0:T(128)S(1)}, f32[32]{0:T(128)S(1)}, u32[]{:S(2)}, u32[]{:S(2)}) collective-permute-start(f32[32]{0:T(128)S(1)} %get-tuple-element.172), channel_id=1, source_target_pairs={{0,1},{1,2},{2,3},{3,4},{4,5},{5,6},{6,7},{7,8},{8,9},{9,10},{10,1... | collective-permute-start | bytes 392 | tf_op jit(solution)/shard_map/ppermute | solution.py:31
  487.7 8.3 %collective-permute-done.19 = f32[32]{0:T(128)S(1)} collective-permute-done((f32[32]{0:T(128)S(1)}, f32[32]{0:T(128)S(1)}, u32[]{:S(2)}, u32[]{:S(2)}) %collective-permute-start.19) | collective-permute-done | bytes 160 | tf_op jit(solution)/shard_map/ppermute | solution.py:34
  (431 shorter events, 289.0 us)
Async XLA Ops:
  2.8 91.2 %collective-permute-start = (f32[7,9,1,512]{3,2,1,0:T(1,128)}, f32[7,9,1,512]{3,2,1,0:T(1,128)}, u32[]{:S(2)}, u32[]{:S(2)}) collective-permute-start(f32[7,9,1,512]{3,2,1,0:T(1,128)} %get-tuple-element.139), channel_id=1, source_target_pairs={{0,8},{8,16},{16,24},{24,32},{32,40},{40,48},{48,56},{56,64},{64,7... | collective-permute-start | bytes 387080 | tf_op jit(solution)/shard_map/ppermute | solution.py:31
  8.8 85.2 %collective-permute-start.1 = (f32[7,9,1,512]{3,2,1,0:T(1,128)}, f32[7,9,1,512]{3,2,1,0:T(1,128)}, u32[]{:S(2)}, u32[]{:S(2)}) collective-permute-start(f32[7,9,1,512]{3,2,1,0:T(1,128)} %get-tuple-element.140), channel_id=1, source_target_pairs={{8,0},{16,8},{24,16},{32,24},{40,32},{48,40},{56,48},{64,56},{72,6... | collective-permute-start | bytes 387080 | tf_op jit(solution)/shard_map/ppermute | solution.py:34
  11.6 25.7 %collective-permute-start.8 = (f32[2,20,32]{2,0,1:T(2,128)S(1)}, f32[2,20,32]{2,0,1:T(2,128)S(1)}, u32[]{:S(2)}, u32[]{:S(2)}) collective-permute-start(f32[2,20,32]{2,0,1:T(2,128)S(1)} %get-tuple-element.156), channel_id=1, source_target_pairs={{0,1},{1,2},{2,3},{3,4},{4,5},{5,6},{6,7},{7,8},{8,9},{9,10},{10,1... | collective-permute-start | bytes 15368 | tf_op jit(solution)/shard_map/ppermute | solution.py:31
  17.8 19.4 %collective-permute-start.9 = (f32[2,20,32]{2,0,1:T(2,128)S(1)}, f32[2,20,32]{2,0,1:T(2,128)S(1)}, u32[]{:S(2)}, u32[]{:S(2)}) collective-permute-start(f32[2,20,32]{2,0,1:T(2,128)S(1)} %get-tuple-element.155), channel_id=1, source_target_pairs={{1,0},{2,1},{3,2},{4,3},{5,4},{6,5},{7,6},{8,7},{9,8},{10,9},{11,1... | collective-permute-start | bytes 15368 | tf_op jit(solution)/shard_map/ppermute | solution.py:34
  23.4 238.5 %copy-start.26 = (s32[1024]{0:T(1024)}, s32[1024]{0:T(1024)S(1)}, u32[]{:S(2)}) copy-start(s32[1024]{0:T(1024)S(1)} %fusion.131) | copy-start | bytes 12292
  23.4 246.0 %copy-start.24 = (s32[1024]{0:T(1024)}, s32[1024]{0:T(1024)S(1)}, u32[]{:S(2)}) copy-start(s32[1024]{0:T(1024)S(1)} %fusion.132) | copy-start | bytes 12292
  96.5 7.1 %collective-permute-start.2 = (f32[7,9,1,512]{3,2,1,0:T(1,128)S(1)}, f32[7,9,1,512]{3,2,1,0:T(1,128)S(1)}, u32[]{:S(2)}, u32[]{:S(2)}) collective-permute-start(f32[7,9,1,512]{3,2,1,0:T(1,128)S(1)} %get-tuple-element.133), channel_id=1, source_target_pairs={{0,8},{8,16},{16,24},{24,32},{32,40},{40,48},{48,56},{56,64},{64,7... | collective-permute-start | bytes 387080 | tf_op jit(solution)/shard_map/ppermute | solution.py:31
  101.6 9.9 %collective-permute-start.3 = (f32[7,9,1,512]{3,2,1,0:T(1,128)S(1)}, f32[7,9,1,512]{3,2,1,0:T(1,128)S(1)}, u32[]{:S(2)}, u32[]{:S(2)}) collective-permute-start(f32[7,9,1,512]{3,2,1,0:T(1,128)S(1)} %get-tuple-element.134), channel_id=1, source_target_pairs={{8,0},{16,8},{24,16},{32,24},{40,32},{48,40},{56,48},{64,56},{72,6... | collective-permute-start | bytes 387080 | tf_op jit(solution)/shard_map/ppermute | solution.py:34
  112.9 4.7 collective-permute-start.4
  114.9 9.9 %collective-permute-start.5 = (f32[7,9,1,512]{3,2,1,0:T(1,128)S(1)}, f32[7,9,1,512]{3,2,1,0:T(1,128)S(1)}, u32[]{:S(2)}, u32[]{:S(2)}) collective-permute-start(f32[7,9,1,512]{3,2,1,0:T(1,128)S(1)} %get-tuple-element.128), channel_id=1, source_target_pairs={{8,0},{16,8},{24,16},{32,24},{40,32},{48,40},{56,48},{64,56},{72,6... | collective-permute-start | bytes 387080 | tf_op jit(solution)/shard_map/ppermute | solution.py:34
  126.3 4.5 collective-permute-start.6
  128.2 9.9 %collective-permute-start.7 = (f32[7,9,1,512]{3,2,1,0:T(1,128)S(1)}, f32[7,9,1,512]{3,2,1,0:T(1,128)S(1)}, u32[]{:S(2)}, u32[]{:S(2)}) collective-permute-start(f32[7,9,1,512]{3,2,1,0:T(1,128)S(1)} %get-tuple-element.122), channel_id=1, source_target_pairs={{8,0},{16,8},{24,16},{32,24},{40,32},{48,40},{56,48},{64,56},{72,6... | collective-permute-start | bytes 387080 | tf_op jit(solution)/shard_map/ppermute | solution.py:34
  150.9 13.1 %all-to-all-start = ((f32[8,1,16128]{2,1,0:T(1,128)}), f32[8,1,16128]{2,1,0:T(1,128)S(1)}, u32[]{:S(2)}, u32[]{:S(2)}) async-start(f32[8,1,16128]{2,1,0:T(1,128)} %reshape.741), calls=%async_computation | async-start | bytes 1032192 | tf_op jit(solution)/shard_map/all_to_all | solution.py:123
  205.6 6.2 %collective-permute-start.10 = (f32[2,8]{1,0:T(2,128)S(1)}, f32[2,8]{1,0:T(2,128)S(1)}, u32[]{:S(2)}, u32[]{:S(2)}) collective-permute-start(f32[2,8]{1,0:T(2,128)S(1)} %get-tuple-element.181), channel_id=1, source_target_pairs={{0,1},{1,2},{2,3},{3,4},{4,5},{5,6},{6,7},{7,8},{8,9},{9,10},{10,1... | collective-permute-start | bytes 200 | tf_op jit(solution)/shard_map/ppermute | solution.py:31
  209.8 10.3 %collective-permute-start.11 = (f32[2,8]{1,0:T(2,128)S(1)}, f32[2,8]{1,0:T(2,128)S(1)}, u32[]{:S(2)}, u32[]{:S(2)}) collective-permute-start(f32[2,8]{1,0:T(2,128)S(1)} %get-tuple-element.182), channel_id=1, source_target_pairs={{1,0},{2,1},{3,2},{4,3},{5,4},{6,5},{7,6},{8,7},{9,8},{10,9},{11,1... | collective-permute-start | bytes 200 | tf_op jit(solution)/shard_map/ppermute | solution.py:34
  232.7 6.7 %collective-permute-start.12 = (f32[2,20,32]{2,0,1:T(2,128)S(1)}, f32[2,20,32]{2,0,1:T(2,128)S(1)}, u32[]{:S(2)}, u32[]{:S(2)}) collective-permute-start(f32[2,20,32]{2,0,1:T(2,128)S(1)} %get-tuple-element.152), channel_id=1, source_target_pairs={{0,1},{1,2},{2,3},{3,4},{4,5},{5,6},{6,7},{7,8},{8,9},{9,10},{10,1... | collective-permute-start | bytes 15368 | tf_op jit(solution)/shard_map/ppermute | solution.py:31
  234.6 10.5 %collective-permute-start.13 = (f32[2,20,32]{2,0,1:T(2,128)S(1)}, f32[2,20,32]{2,0,1:T(2,128)S(1)}, u32[]{:S(2)}, u32[]{:S(2)}) collective-permute-start(f32[2,20,32]{2,0,1:T(2,128)S(1)} %get-tuple-element.151), channel_id=1, source_target_pairs={{1,0},{2,1},{3,2},{4,3},{5,4},{6,5},{7,6},{8,7},{9,8},{10,9},{11,1... | collective-permute-start | bytes 15368 | tf_op jit(solution)/shard_map/ppermute | solution.py:34
  297.8 31.1 %collective-permute-start.14 = (f32[2,20,32]{2,0,1:T(2,128)S(1)}, f32[2,20,32]{2,0,1:T(2,128)S(1)}, u32[]{:S(2)}, u32[]{:S(2)}) collective-permute-start(f32[2,20,32]{2,0,1:T(2,128)S(1)} %get-tuple-element.148), channel_id=1, source_target_pairs={{0,1},{1,2},{2,3},{3,4},{4,5},{5,6},{6,7},{7,8},{8,9},{9,10},{10,1... | collective-permute-start | bytes 15368 | tf_op jit(solution)/shard_map/ppermute | solution.py:31
  300.0 28.9 %collective-permute-start.15 = (f32[2,20,32]{2,0,1:T(2,128)S(1)}, f32[2,20,32]{2,0,1:T(2,128)S(1)}, u32[]{:S(2)}, u32[]{:S(2)}) collective-permute-start(f32[2,20,32]{2,0,1:T(2,128)S(1)} %get-tuple-element.147), channel_id=1, source_target_pairs={{1,0},{2,1},{3,2},{4,3},{5,4},{6,5},{7,6},{8,7},{9,8},{10,9},{11,1... | collective-permute-start | bytes 15368 | tf_op jit(solution)/shard_map/ppermute | solution.py:34
  389.2 38.1 %collective-permute-start.16 = (f32[2,20,32]{2,0,1:T(2,128)S(1)}, f32[2,20,32]{2,0,1:T(2,128)S(1)}, u32[]{:S(2)}, u32[]{:S(2)}) collective-permute-start(f32[2,20,32]{2,0,1:T(2,128)S(1)} %get-tuple-element.144), channel_id=1, source_target_pairs={{0,1},{1,2},{2,3},{3,4},{4,5},{5,6},{6,7},{7,8},{8,9},{9,10},{10,1... | collective-permute-start | bytes 15368 | tf_op jit(solution)/shard_map/ppermute | solution.py:31
  396.9 30.5 %collective-permute-start.17 = (f32[2,20,32]{2,0,1:T(2,128)S(1)}, f32[2,20,32]{2,0,1:T(2,128)S(1)}, u32[]{:S(2)}, u32[]{:S(2)}) collective-permute-start(f32[2,20,32]{2,0,1:T(2,128)S(1)} %get-tuple-element.143), channel_id=1, source_target_pairs={{1,0},{2,1},{3,2},{4,3},{5,4},{6,5},{7,6},{8,7},{9,8},{10,9},{11,1... | collective-permute-start | bytes 15368 | tf_op jit(solution)/shard_map/ppermute | solution.py:34
  422.5 81.9 %all-to-all-start.1 = ((f32[7,72,256]{2,0,1:T(8,128)}), f32[7,72,256]{2,0,1:T(8,128)S(1)}, u32[]{:S(2)}, u32[]{:S(2)}) async-start(f32[7,72,256]{2,0,1:T(8,128)} %copy.387), calls=%async_computation.1 | async-start | bytes 1179648 | tf_op jit(solution)/shard_map/all_to_all | solution.py:130
  478.0 9.7 %collective-permute-start.18 = (f32[32]{0:T(128)S(1)}, f32[32]{0:T(128)S(1)}, u32[]{:S(2)}, u32[]{:S(2)}) collective-permute-start(f32[32]{0:T(128)S(1)} %get-tuple-element.172), channel_id=1, source_target_pairs={{0,1},{1,2},{2,3},{3,4},{4,5},{5,6},{6,7},{7,8},{8,9},{9,10},{10,1... | collective-permute-start | bytes 392 | tf_op jit(solution)/shard_map/ppermute | solution.py:31
  485.8 10.3 %collective-permute-start.19 = (f32[32]{0:T(128)S(1)}, f32[32]{0:T(128)S(1)}, u32[]{:S(2)}, u32[]{:S(2)}) collective-permute-start(f32[32]{0:T(128)S(1)} %get-tuple-element.171), channel_id=1, source_target_pairs={{1,0},{2,1},{3,2},{4,3},{5,4},{6,5},{7,6},{8,7},{9,8},{10,9},{11,1... | collective-permute-start | bytes 392 | tf_op jit(solution)/shard_map/ppermute | solution.py:34
  (84 other events, 1348.0 us)
where the time goes:
time: 515 us; the launch traced here: 506 us
  local copies, waits for them, and re-layouts  328 us (64%)
  starting transfers between devices  81 us (16%)
  waiting for transfers between devices  49.7 us (10%)
  other arithmetic  44.1 us (9%)
    gather x48, local copies, waits for them, and re-layouts, local(): beside_all = beside_all + jnp.take(extended, neighbor_index[link], axis=2)  205 us
    ppermute x10, starting transfers between devices, extended_2(): lax.ppermute(lax.slice_in_dim(block, block.shape[dim] - width, None, axis...  44.8 us
    ppermute x10, waiting for transfers between devices, extended_2(): lax.ppermute(lax.slice_in_dim(block, 0, width, axis=dim), axis, backward)  44.8 us
    ppermute x10, starting transfers between devices, extended_2(): lax.ppermute(lax.slice_in_dim(block, 0, width, axis=dim), axis, backward)  23.4 us
    scatter-add x1, local copies, waits for them, and re-layouts, surface(): columns = columns.at[0, -1].add(-HEAT_BACK * heat_flux)  23.1 us
    scatter-add x2, local copies, waits for them, and re-layouts, surface(): columns = columns.at[3, -1].add(-MOIST_BACK * fresh_flux)  23.1 us
    unnamed x175, local copies, waits for them, and re-layouts  18.7 us
    gather x8, local copies, waits for them, and re-layouts, local(): jnp.take(nearby, indices[link], axis=1)  12 us
  transfers between devices with their start and end apart: 22, of which 7 were waited for; matrix products, arithmetic and copies ran while one was open for 36% of the time, Pallas kernels for 0%

commit v1 on v0

v1 whole, which is shorter than its diff:
```python
import functools

import jax
import jax.numpy as jnp
from jax import lax
from jax.experimental import pallas as pl
from jax.experimental.pallas import tpu as pltpu
from jax.sharding import PartitionSpec as P

MESH = pl.DeviceIdType.MESH
F32 = jnp.float32
BF16 = jnp.bfloat16

FIELDS = 7
LEV = 72
NLEV = 9
ROWS = 4
QS = 4
DYN_STEPS = 4
PHYS_ITERS = 3
CONV_ITERS = 24
OLEV = 20
OSTEPS = 4
NBR = 6
NW = 4
PARTS = 3
OROW = 48
NT = 12
OCEAN_SPREAD = 0.6
OCEAN_VERTICAL = 0.2
HEAT_COEF = 0.5
MOIST_COEF = 0.5
HEAT_BACK = 0.3
MOIST_BACK = 0.3
OCEAN_FORCE = 0.3

GROUPS = ((0, 4), (4, 3))
HSUB = 16


def iota(shape, dim):
    return lax.broadcasted_iota(jnp.int32, shape, dim)


def kernel(
    n_atm,
    n_ocn,
    atm, ld, lw, vr, cr, skin, trig, order, ocean, nbr, fsrc, fw, ssrc, sw,
    out_atm, out_ocean, out_surf,
    ld_s, lw_s, vr_s, cr_s, skin_v, trig_v, order_v, ssrc_v, sw_v,
    nb, d0, d1, coef,
    sa0, ra0, pa0, ba0, sa1, ra1, pa1, ba1,
    xa, xb, out_v,
    oc_l, oc_o, oc_r, nbr_e, fsrc_e, fw_e,
    st, hs, mm, ff, uu, oout, sout,
    fl, fl_l, fl_r,
    local_sem, halo_send, halo_recv, oh_send, oh_recv,
    a_send, a_recv, b_send, b_recv, self_sem, f_send, f_recv, out_sem,
):
    a = lax.axis_index("atm")
    o = lax.axis_index("ocn")
    dev = a * n_ocn + o
    up = lax.rem(a + n_atm - 1, n_atm)
    down = lax.rem(a + 1, n_atm)
    total = n_atm * n_ocn
    left = lax.rem(dev + total - 1, total)
    right = lax.rem(dev + 1, total)
    left_id = (left // n_ocn, lax.rem(left, n_ocn))
    right_id = (right // n_ocn, lax.rem(right, n_ocn))
    peers = [lax.rem(o + d, n_ocn) for d in range(1, n_ocn)]

    fills = [
        (ld, ld_s), (lw, lw_s), (vr, vr_s), (cr, cr_s),
        (skin, skin_v), (trig, trig_v), (order, order_v), (ssrc, ssrc_v), (sw, sw_v),
        (atm, nb.at[1]), (ocean, oc_o),
        (nbr, nbr_e.at[:, pl.ds(256, 1024)]),
        (fsrc, fsrc_e.at[:, pl.ds(256, 1024)]),
        (fw, fw_e.at[:, pl.ds(256, 1024)]),
    ]
    fills = [
        pltpu.make_async_copy(src, dst, local_sem.at[i]) for i, (src, dst) in enumerate(fills)
    ]
    for copy in fills:
        copy.start()

    barrier = pltpu.get_barrier_semaphore()
    partners = [(up, o), (down, o), left_id, right_id] + [(a, p) for p in peers]
    for partner in partners:
        pl.semaphore_signal(barrier, inc=1, device_id=partner, device_id_type=MESH)
    pl.semaphore_wait(barrier, len(partners))

    def remote(src, dst, send, recv, device):
        return pltpu.make_async_remote_copy(
            src_ref=src, dst_ref=dst, send_sem=send, recv_sem=recv,
            device_id=device, device_id_type=MESH,
        )

    def halo(g):
        f0, nf = GROUPS[g]
        rows = pl.ds(f0 * NLEV * HSUB, nf * NLEV * HSUB)
        return [
            remote(atm.at[rows], nb.at[0, rows], halo_send.at[g, 0], halo_recv.at[g, 0], (down, o)),
            remote(atm.at[rows], nb.at[2, rows], halo_send.at[g, 1], halo_recv.at[g, 1], (up, o)),
        ]

    halos = [halo(0), halo(1)]
    for copy in halos[0]:
        copy.start()

    ocean3 = ocean.reshape(OLEV, 16, 128)
    last, first = pl.ds(768, 256), pl.ds(0, 256)
    low, high = pl.ds(0, 256), pl.ds(1280, 256)
    edge = [
        (ocean3.at[:, pl.ds(8, 8)], oc_l.reshape(OLEV, 8, 128), right_id),
        (nbr.at[:, last], nbr_e.at[:, low], right_id),
        (fsrc.at[:, last], fsrc_e.at[:, low], right_id),
        (fw.at[:, last], fw_e.at[:, low], right_id),
        (ocean3.at[:, pl.ds(0, 8)], oc_r.reshape(OLEV, 8, 128), left_id),
        (nbr.at[:, first], nbr_e.at[:, high], left_id),
        (fsrc.at[:, first], fsrc_e.at[:, high], left_id),
        (fw.at[:, first], fw_e.at[:, high], left_id),
    ]
    edges = [
        remote(src, dst, oh_send.at[i], oh_recv.at[i], device)
        for i, (src, dst, device) in enumerate(edge)
    ]
    for copy in edges:
        copy.start()
    for copy in halos[1]:
        copy.start()

    for copy in fills:
        copy.wait()

    hit = jnp.where(trig_v[...] > 0, order_v[...], -1).astype(F32)
    hit = jnp.concatenate([hit, jnp.full((6, 128), -1.0, F32)], axis=0)
    hit = jnp.transpose(hit, (1, 0))
    lane = iota((128, 128), 1)
    active = []
    for half in range(2):
        column = (lane + 128 * half).astype(F32)
        mark = jnp.where(hit[:, 0:1] == column, 1.0, 0.0) + jnp.where(hit[:, 1:2] == column, 1.0, 0.0)
        active.append(jnp.sum(mark, axis=0, keepdims=True))

    for copy in edges:
        copy.wait_recv()

    unused = jnp.zeros((4, 128), F32)
    for u in range(NT):
        for f in range(2):
            if u < 2:
                piece = oc_l[pl.ds((u + 2) * 2 + f, OLEV, stride=8), :]
            elif u < 10:
                piece = oc_o[pl.ds((u - 2) * 2 + f, OLEV, stride=16), :]
            else:
                piece = oc_r[pl.ds((u - 10) * 2 + f, OLEV, stride=8), :]
            st[pl.ds(u * OROW + f * 24, OLEV), :] = piece
            st[pl.ds(u * OROW + f * 24 + OLEV, 4), :] = unused

    def build(u, carry):
        at = pl.multiple_of(u * 128, 128)
        k = iota((192, 128), 0) + 96
        base = iota((1, 128), 1) + 128
        count = jnp.zeros((192, 128), F32)
        for j in range(NBR):
            target = nbr_e[pl.ds(j, 1), pl.ds(at, 128)] + base
            count = count + jnp.where(k == target, 1.0, 0.0)
        mm[u - 1, pl.ds(0, 96), :] = jnp.zeros((96, 128), BF16)
        mm[u - 1, pl.ds(96, 192), :] = count.astype(BF16)
        mm[u - 1, pl.ds(288, 96), :] = jnp.zeros((96, 128), BF16)
        return carry

    lax.fori_loop(1, NT - 1, build, 0)

    level_row = lax.rem(iota((OROW, 128), 0), 24)

    def spread(force):
        def split(u, carry):
            rest = st[pl.ds(pl.multiple_of(u * OROW, OROW), OROW), :]
            for part in range(PARTS):
                piece = rest.astype(BF16)
                hs[u, pl.ds(part * OROW, OROW), :] = piece
                rest = rest - piece.astype(F32)
            return carry

        lax.fori_loop(0, NT, split, 0)

        def tile(u, carry):
            source = jnp.concatenate([hs[u - 1], hs[u], hs[u + 1]], axis=1)
            sums = jnp.dot(source, mm[u - 1], preferred_element_type=F32)
            around = sums[0:OROW]
            for part in range(1, PARTS):
                around = around + sums[part * OROW : (part + 1) * OROW]
            rows = pl.ds(pl.multiple_of(u * OROW, OROW), OROW)
            here = st[rows, :]
            here = here + OCEAN_SPREAD * (around * (1.0 / 6.0) - here)
            above = jnp.where(level_row == 0, here, pltpu.roll(here, 1, 0))
            below = jnp.where(level_row == OLEV - 1, here, pltpu.roll(here, OROW - 1, 0))
            here = here + OCEAN_VERTICAL * (above + below - 2.0 * here)
            if force:
                here = here + ff[pl.ds(pl.multiple_of(u * OROW, OROW), OROW), :]
            st[rows, :] = jnp.where(level_row < OLEV, here, 0.0)
            return carry

        lax.fori_loop(1, NT - 1, tile, 0)

    spread(False)

    keep_up = jnp.where(a > 0, 1.0, 0.0).astype(F32)
    keep_down = jnp.where(a < n_atm - 1, 1.0, 0.0).astype(F32)
    sends = (sa0, sa1)
    takes = (ra0, ra1)
    packs = (pa0, pa1)
    backs = (ba0, ba1)

    def dynamics(g):
        f0, nf = GROUPS[g]
        n = nf * NLEV
        sub = lax.rem(iota((n, 128), 0), NLEV)
        diff = jnp.zeros((n, 128), F32)
        wind = jnp.zeros((n, 128), F32)
        for l in range(NLEV):
            diff = jnp.where(sub == l, ld_s[l], diff)
            wind = jnp.where(sub == l, lw_s[l], wind)
        coef[0, pl.ds(0, n), :] = 1.0 - 4.0 * diff
        coef[1, pl.ds(0, n), :] = diff
        coef[2, pl.ds(0, n), :] = diff - 0.5 * wind
        coef[3, pl.ds(0, n), :] = diff + 0.5 * wind
        for b in range(3):
            for r in range(ROWS):
                for q in range(QS):
                    piece = nb[b, pl.ds(f0 * NLEV * HSUB + 4 * q + r, n, stride=HSUB), :]
                    if b == 0:
                        piece = piece * keep_up
                    if b == 2:
                        piece = piece * keep_down
                    d0[b * ROWS + r, q, pl.ds(0, n), :] = piece
        lane = iota((n, 128), 1)
        bufs = (d0, d1)
        for step in range(1, DYN_STEPS + 1):
            src, dst = bufs[(step - 1) % 2], bufs[step % 2]

            def row(i, carry):
                here = [src[i, q, pl.ds(0, n), :] for q in range(QS)]
                to_east = [pltpu.roll(x, 1, 1) for x in here]
                to_west = [pltpu.roll(x, 127, 1) for x in here]
                for q in range(QS):
                    west = jnp.where(lane == 0, to_east[(q - 1) % QS], to_east[q])
                    east = jnp.where(lane == 127, to_west[(q + 1) % QS], to_west[q])
                    beside = src[i - 1, q, pl.ds(0, n), :] + src[i + 1, q, pl.ds(0, n), :]
                    new = (
                        coef[0, pl.ds(0, n), :] * here[q]
                        + coef[1, pl.ds(0, n), :] * beside
                        + coef[2, pl.ds(0, n), :] * east
                        + coef[3, pl.ds(0, n), :] * west
                    )
                    if step == DYN_STEPS:
                        sends[g][(i - ROWS) * 2 + q // 2, pl.ds((q % 2) * n, n), :] = new
                    else:
                        keep = jnp.where(i < ROWS, keep_up, jnp.where(i >= 2 * ROWS, keep_down, 1.0))
                        dst[i, q, pl.ds(0, n), :] = new * keep
                return carry

            lax.fori_loop(step, 3 * ROWS - step, row, 0)

    def exchange(src, dst, send, recv, g):
        copies = [
            remote(src.at[p], dst.at[o], send.at[g, p], recv.at[g, o], (a, p)) for p in peers
        ]
        own = pltpu.make_async_copy(src.at[o], dst.at[o], self_sem.at[g])
        for copy in copies:
            copy.start()
        own.start()
        arrivals = [
            remote(src.at[p], dst.at[p], send.at[g, p], recv.at[g, p], (a, p)) for p in peers
        ]
        return copies, own, arrivals

    def landed(handle):
        copies, own, arrivals = handle
        own.wait()
        for copy in arrivals:
            copy.wait_recv()

    out_there = []
    for g in range(2):
        for copy in halos[g]:
            copy.wait_recv()
        dynamics(g)
        out_there.append(exchange(sends[g], takes[g], a_send, a_recv, g))

    def physics(g):
        f0, nf = GROUPS[g]
        n = 2 * nf
        x = (xa, xb)[g]
        sub = iota((n, 128), 0)
        field = lax.rem(sub, nf)
        mix = jnp.zeros((n, 128), F32)
        rate = jnp.zeros((n, 128), F32)
        for f in range(nf):
            mix = jnp.where(field == f, vr_s[f0 + f], mix)
            rate = jnp.where(field == f, cr_s[f0 + f], rate)
        rate = rate * jnp.where(sub < nf, active[0], active[1])

        for lev in range(LEV):
            x[lev, pl.ds(0, n), :] = takes[g][lev // NLEV, pl.ds(lev % NLEV, n, stride=NLEV), :]

        def vertical(i, carry):
            here = x[0, pl.ds(0, n), :]
            above = here
            for lev in range(LEV):
                below = x[lev + 1, pl.ds(0, n), :] if lev < LEV - 1 else here
                x[lev, pl.ds(0, n), :] = here + mix * (above + below - 2.0 * here)
                above, here = here, below
            return carry

        lax.fori_loop(0, PHYS_ITERS, vertical, 0)

        def convect(i, carry):
            here = x[0, pl.ds(0, n), :]
            came = jnp.zeros((n, 128), F32)
            for lev in range(LEV - 1):
                below = x[lev + 1, pl.ds(0, n), :]
                transfer = rate * jnp.tanh(below - here)
                x[lev, pl.ds(0, n), :] = here + transfer - came
                came, here = transfer, below
            x[LEV - 1, pl.ds(0, n), :] = here - came
            return carry

        lax.fori_loop(0, CONV_ITERS, convect, 0)

    def pack(g):
        nf = GROUPS[g][1]
        n = 2 * nf
        x = (xa, xb)[g]
        for lev in range(LEV):
            packs[g][lev // NLEV, pl.ds(lev % NLEV, n, stride=NLEV), :] = x[lev, pl.ds(0, n), :]

    landed(out_there[0])
    physics(0)

    fl[...] = jnp.zeros((8, 128), F32)
    for half in range(2):
        low_row = [xa[LEV - 1, pl.ds(half * 4 + f, 1), :] for f in range(4)]
        speed = jnp.sqrt(1.0 + low_row[1] * low_row[1] + low_row[2] * low_row[2])
        heat = HEAT_COEF * speed * (low_row[0] - skin_v[pl.ds(half, 1), :])
        fresh = MOIST_COEF * speed * low_row[3]
        xa[LEV - 1, pl.ds(half * 4, 1), :] = low_row[0] - HEAT_BACK * heat
        xa[LEV - 1, pl.ds(half * 4 + 3, 1), :] = low_row[3] - MOIST_BACK * fresh
        fl[pl.ds(2 * half, 1), :] = heat
        fl[pl.ds(2 * half + 1, 1), :] = fresh
    fluxes = [
        remote(fl, fl_l, f_send.at[0], f_recv.at[0], right_id),
        remote(fl, fl_r, f_send.at[1], f_recv.at[1], left_id),
    ]
    for copy in fluxes:
        copy.start()
    pack(0)
    back_home = [exchange(packs[0], backs[0], b_send, b_recv, 0)]
    landed(out_there[1])
    physics(1)
    pack(1)
    back_home.append(exchange(packs[1], backs[1], b_send, b_recv, 1))

    for copy in fluxes:
        copy.wait_recv()
    near = jnp.concatenate(
        [
            fl_l[pl.ds(2, 1), :], fl[pl.ds(0, 1), :], fl[pl.ds(2, 1), :], fl_r[pl.ds(0, 1), :],
            fl_l[pl.ds(3, 1), :], fl[pl.ds(1, 1), :], fl[pl.ds(3, 1), :], fl_r[pl.ds(1, 1), :],
        ],
        axis=0,
    )
    sub8 = iota((8, 128), 0)
    chunk = lax.rem(sub8, 4)
    ff[...] = jnp.zeros(ff.shape, F32)
    for u in range(1, NT - 1):
        at = pl.ds(u * 128, 128)
        acc = jnp.zeros((8, 128), F32)
        for link in range(NW):
            source = fsrc_e[pl.ds(link, 1), at] - (dev * 256 - 128)
            source = jnp.broadcast_to(source, (8, 128))
            picked = jnp.take_along_axis(near, source & 127, axis=1, mode="promise_in_bounds")
            picked = jnp.where((source >> 7) == chunk, picked, 0.0)
            acc = acc + fw_e[pl.ds(link, 1), at] * picked
        ff[pl.ds(u * OROW, 1), :] = OCEAN_FORCE * jnp.sum(acc[0:4], axis=0, keepdims=True)
        ff[pl.ds(u * OROW + 24, 1), :] = OCEAN_FORCE * jnp.sum(acc[4:8], axis=0, keepdims=True)
    for u in range(1, NT - 1):
        for f in range(2):
            row = pl.ds(u * OROW + 24 * f, 1)
            st[row, :] = st[row, :] + ff[row, :]

    def ocean_step(i, carry):
        spread(True)
        return carry

    lax.fori_loop(1, OSTEPS, ocean_step, 0)

    for u in range(2, 10):
        for f in range(2):
            oout[pl.ds((u - 2) * 2 + f, OLEV, stride=16), :] = st[pl.ds(u * OROW + f * 24, OLEV), :]
    ocean_copy = pltpu.make_async_copy(oout, out_ocean, out_sem.at[0])
    ocean_copy.start()

    uu[...] = jnp.zeros(uu.shape, F32)
    for u in range(1, NT - 1):
        uu[pl.ds(u, 1), :] = st[pl.ds(u * OROW, 1), :]
    top = (uu[pl.ds(0, 8), :], uu[pl.ds(8, 8), :])
    for half in range(2):
        at = pl.ds(half * 128, 128)
        acc = jnp.zeros((8, 128), F32)
        for link in range(NW):
            source = ssrc_v[pl.ds(link, 1), at] - (dev * 1024 - 256)
            source = jnp.broadcast_to(source, (8, 128))
            weight = sw_v[pl.ds(link, 1), at]
            for part in range(2):
                picked = jnp.take_along_axis(top[part], source & 127, axis=1, mode="promise_in_bounds")
                picked = jnp.where((source >> 7) == sub8 + 8 * part, picked, 0.0)
                acc = acc + weight * picked
        sout[pl.ds(half, 1), :] = jnp.sum(acc, axis=0, keepdims=True)
    surf_copy = pltpu.make_async_copy(sout, out_surf, out_sem.at[1])
    surf_copy.start()

    out_copies = [ocean_copy, surf_copy]
    for g in range(2):
        f0, nf = GROUPS[g]
        n = nf * NLEV
        landed(back_home[g])
        for r in range(ROWS):
            for q in range(QS):
                piece = backs[g][2 * r + q // 2, pl.ds((q % 2) * n, n), :]
                out_v[pl.ds(f0 * NLEV * HSUB + 4 * q + r, n, stride=HSUB), :] = piece
        rows = pl.ds(f0 * NLEV * HSUB, n * HSUB)
        copy = pltpu.make_async_copy(out_v.at[rows], out_atm.at[rows], out_sem.at[2 + g])
        copy.start()
        out_copies.append(copy)

    for copy in halos[0] + halos[1] + edges + fluxes:
        copy.wait_send()
    for copies, own, arrivals in out_there + back_home:
        for copy in copies:
            copy.wait_send()
    for copy in out_copies:
        copy.wait()


def local(n_atm, n_ocn, atm_state, level_diffusion, level_wind, vertical_rate, convective_rate,
          ocean_skin, trigger, group_order, ocean_state, ocean_neighbors, flux_sources,
          flux_weights, surface_sources, surface_weights):
    atm = atm_state.reshape(FIELDS, NLEV, ROWS, QS, 128).transpose(0, 1, 3, 2, 4).reshape(1008, 128)
    ocean = ocean_state.transpose(1, 0, 2).reshape(OLEV, 2, 8, 128).transpose(0, 2, 1, 3).reshape(320, 128)
    hbm = pl.BlockSpec(memory_space=pltpu.HBM)
    dma = pltpu.SemaphoreType.DMA

    def vmem(*shape, dtype=F32):
        return pltpu.VMEM(shape, dtype)

    new_atm, new_ocean, surf = pl.pallas_call(
        functools.partial(kernel, n_atm, n_ocn),
        out_shape=(
            jax.ShapeDtypeStruct((1008, 128), F32),
            jax.ShapeDtypeStruct((320, 128), F32),
            jax.ShapeDtypeStruct((2, 128), F32),
        ),
        in_specs=[hbm] * 14,
        out_specs=(hbm,) * 3,
        scratch_shapes=[
            pltpu.SMEM((NLEV,), F32), pltpu.SMEM((NLEV,), F32),
            pltpu.SMEM((FIELDS,), F32), pltpu.SMEM((FIELDS,), F32),
            vmem(2, 128), vmem(2, 128, dtype=jnp.int32), vmem(2, 128, dtype=jnp.int32),
            vmem(4, 256, dtype=jnp.int32), vmem(4, 256),
            vmem(3, 1008, 128), vmem(12, QS, 40, 128), vmem(12, QS, 40, 128), vmem(4, 40, 128),
            vmem(8, 72, 128), vmem(8, 72, 128), vmem(8, 72, 128), vmem(8, 72, 128),
            vmem(8, 56, 128), vmem(8, 56, 128), vmem(8, 56, 128), vmem(8, 56, 128),
            vmem(LEV, 8, 128), vmem(LEV, 8, 128), vmem(1008, 128),
            vmem(160, 128), vmem(320, 128), vmem(160, 128),
            vmem(NBR, 1536, dtype=jnp.int32), vmem(NW, 1536, dtype=jnp.int32), vmem(NW, 1536),
            vmem(NT * OROW, 128), vmem(NT, PARTS * OROW, 128, dtype=BF16),
            vmem(NT - 2, 384, 128, dtype=BF16), vmem(NT * OROW, 128), vmem(16, 128),
            vmem(320, 128), vmem(2, 128),
            vmem(8, 128), vmem(8, 128), vmem(8, 128),
            dma((14,)), dma((2, 2)), dma((2, 2)), dma((8,)), dma((8,)),
            dma((2, 8)), dma((2, 8)), dma((2, 8)), dma((2, 8)), dma((2,)),
            dma((2,)), dma((2,)), dma((4,)),
        ],
        compiler_params=pltpu.CompilerParams(
            collective_id=0, has_side_effects=True, vmem_limit_bytes=40 * 1024 * 1024
        ),
    )(
        atm, level_diffusion, level_wind, vertical_rate, convective_rate,
        ocean_skin.reshape(2, 128), trigger.reshape(2, 128), group_order.reshape(2, 128),
        ocean, ocean_neighbors, flux_sources, flux_weights, surface_sources, surface_weights,
    )
    new_atm = new_atm.reshape(FIELDS, NLEV, QS, ROWS, 128).transpose(0, 1, 3, 2, 4)
    new_ocean = new_ocean.reshape(OLEV, 8, 2, 128).transpose(0, 2, 1, 3).reshape(OLEV, 2, 1024)
    return (
        new_atm.reshape(FIELDS, NLEV, ROWS, QS * 128),
        new_ocean.transpose(1, 0, 2),
        surf.reshape(256),
    )


def solution(mesh):
    both = ("atm", "ocn")
    return jax.shard_map(
        functools.partial(local, mesh.shape["atm"], mesh.shape["ocn"]),
        mesh=mesh,
        in_specs=(
            P(None, "ocn", "atm", None), P("ocn"), P("ocn"), P(), P(),
            P(both), P(both), P(both), P(None, None, both),
            P(None, both), P(None, both), P(None, both), P(None, both), P(None, both),
        ),
        out_specs=(P(None, "ocn", "atm", None), P(None, None, both), P(both)),
        check_vma=False,
    )
```

time: 515 us -> 58.7 us (0.11)
  the two profiles are of different devices: /device:TPU:127 before, /device:TPU:16 now
where the time goes in v1:
time: 58.7 us; the launch traced here: 58.2 us
  Pallas kernels  46.7 us (80%)
  local copies, waits for them, and re-layouts  10.8 us (18%)
  between operations  0.68 us (1%)
    pallas_call x1, Pallas kernels, local(): pl.pallas_call(functools.partial(kernel, n_atm, n_ocn), out_shape=(jax.Sh...  46.7 us
    unnamed x31, local copies, waits for them, and re-layouts  10.8 us

profile of v1, /device:TPU:16, one launch (start us, length us, event | category | flops | bytes accessed | tf_op | source)
XLA Modules:
  0.0 58.2 jit_solution(17263858617126825631)
XLA Ops:
  0.6 0.0 copy-start.6
  0.6 0.0 copy-start.5
  0.7 0.0 copy-start.7
  0.7 0.7 %copy-done.6 = f32[4,256]{1,0:T(4,128)S(1)} copy-done((f32[4,256]{1,0:T(4,128)S(1)}, f32[4,256]{1,0:T(4,128)}, u32[]{:S(2)}) %copy-start.6) | copy-done | bytes 4120
  1.3 0.0 copy-done.5
  1.3 0.0 copy-done.7
  1.3 0.0 copy-start
  1.4 1.0 %copy-done = f32[7,9,4,512]{3,2,1,0:T(4,128)S(1)} copy-done((f32[7,9,4,512]{3,2,1,0:T(4,128)S(1)}, f32[7,9,4,512]{3,2,1,0:T(4,128)}, u32[]{:S(2)}) %copy-start) | copy-done | bytes 516120
  2.4 0.0 copy-start.1
  2.4 0.9 %copy-done.1 = f32[2,20,1024]{2,0,1:T(2,128)S(1)} copy-done((f32[2,20,1024]{2,0,1:T(2,128)S(1)}, f32[2,20,1024]{2,0,1:T(2,128)}, u32[]{:S(2)}) %copy-start.1) | copy-done | bytes 163864
  3.3 0.0 copy-start.2
  3.3 0.8 %copy-done.2 = s32[6,1024]{1,0:T(8,128)S(1)} copy-done((s32[6,1024]{1,0:T(8,128)S(1)}, s32[6,1024]{1,0:T(8,128)}, u32[]{:S(2)}) %copy-start.2) | copy-done | bytes 24600
  4.1 0.7 %copy-done.3 = s32[4,1024]{1,0:T(4,128)S(1)} copy-done((s32[4,1024]{1,0:T(4,128)S(1)}, s32[4,1024]{1,0:T(4,128)}, u32[]{:S(2)}) %copy-start.3) | copy-done | bytes 16408
  4.8 0.7 %copy-done.4 = f32[4,1024]{1,0:T(4,128)S(1)} copy-done((f32[4,1024]{1,0:T(4,128)S(1)}, f32[4,1024]{1,0:T(4,128)}, u32[]{:S(2)}) %copy-start.4) | copy-done | bytes 16408
  5.5 0.7 %copy-done.8 = s32[256]{0:T(256)S(1)} copy-done((s32[256]{0:T(256)S(1)}, s32[256]{0:T(256)}, u32[]{:S(2)}) %copy-start.8) | copy-done | bytes 1048
  6.2 0.7 %copy-done.9 = s32[256]{0:T(256)S(1)} copy-done((s32[256]{0:T(256)S(1)}, s32[256]{0:T(256)}, u32[]{:S(2)}) %copy-start.9) | copy-done | bytes 1048
  6.9 0.7 %copy-done.10 = f32[9]{0:T(128)S(1)} copy-done((f32[9]{0:T(128)S(1)}, f32[9]{0:T(128)}, u32[]{:S(2)}) %copy-start.10) | copy-done | bytes 60
  7.5 0.7 %copy-done.11 = f32[9]{0:T(128)S(1)} copy-done((f32[9]{0:T(128)S(1)}, f32[9]{0:T(128)}, u32[]{:S(2)}) %copy-start.11) | copy-done | bytes 60
  8.2 0.7 %copy-done.12 = f32[7]{0:T(128)S(1)} copy-done((f32[7]{0:T(128)S(1)}, f32[7]{0:T(128)}, u32[]{:S(2)}) %copy-start.12) | copy-done | bytes 52
  8.8 0.7 %copy-done.13 = f32[7]{0:T(128)S(1)} copy-done((f32[7]{0:T(128)S(1)}, f32[7]{0:T(128)}, u32[]{:S(2)}) %copy-start.13) | copy-done | bytes 52
  9.5 46.7 %shard_map.157 = (f32[1008,128]{1,0:T(8,128)S(1)}, f32[320,128]{1,0:T(8,128)S(1)}, f32[2,128]{1,0:T(2,128)S(1)}) custom-call(f32[1008,128]{1,0:T(8,128)S(1)} %bitcast.28, f32[9]{0:T(128)S(1)} %copy-done.10, f32[9]{0:T(128)S(1)} %copy-done.11, f32[7]{0:T(128)S(1)} %copy-done.12, f32[7]{0:T(128)S(1)} %copy-done.13, f32[2,128]{1,0:T(2,128)S(1)} %bitcast.32, ...), custom_call_target="tpu_custom_call" | custom-call | tf_op jit(solution)/shard_map/pallas_call | solution.py:458
  56.2 0.8 %copy.23 = f32[7,9,4,512]{3,2,1,0:T(4,128)} copy(f32[7,9,4,512]{3,2,1,0:T(4,128)S(1)} %bitcast.29) | data formatting | bytes 1032192
  57.0 0.7 %copy.24 = f32[2,20,1024]{2,0,1:T(2,128)} copy(f32[2,20,1024]{2,0,1:T(2,128)S(1)} %bitcast.30) | data formatting | bytes 327680
  57.7 0.6 copy.25
  (8 shorter events, 0.0 us)
Async XLA Ops:
  0.6 0.7 %copy-start.6 = (f32[4,256]{1,0:T(4,128)S(1)}, f32[4,256]{1,0:T(4,128)}, u32[]{:S(2)}) copy-start(f32[4,256]{1,0:T(4,128)} %sw.1) | copy-start | bytes 12292
  0.6 0.7 %copy-start.5 = (s32[4,256]{1,0:T(4,128)S(1)}, s32[4,256]{1,0:T(4,128)}, u32[]{:S(2)}) copy-start(s32[4,256]{1,0:T(4,128)} %ssrc.1) | copy-start | bytes 12292
  0.7 0.7 %copy-start.7 = (f32[256]{0:T(256)S(1)}, f32[256]{0:T(256)}, u32[]{:S(2)}) copy-start(f32[256]{0:T(256)} %param.19) | copy-start | bytes 3076
  1.3 1.0 %copy-start = (f32[7,9,4,512]{3,2,1,0:T(4,128)S(1)}, f32[7,9,4,512]{3,2,1,0:T(4,128)}, u32[]{:S(2)}) copy-start(f32[7,9,4,512]{3,2,1,0:T(4,128)} %param.14) | copy-start | bytes 1548292
  2.4 0.9 %copy-start.1 = (f32[2,20,1024]{2,0,1:T(2,128)S(1)}, f32[2,20,1024]{2,0,1:T(2,128)}, u32[]{:S(2)}) copy-start(f32[2,20,1024]{2,0,1:T(2,128)} %param.22) | copy-start | bytes 491524
  3.3 0.8 %copy-start.2 = (s32[6,1024]{1,0:T(8,128)S(1)}, s32[6,1024]{1,0:T(8,128)}, u32[]{:S(2)}) copy-start(s32[6,1024]{1,0:T(8,128)} %nbr.1) | copy-start | bytes 73732
  4.1 0.7 %copy-start.3 = (s32[4,1024]{1,0:T(4,128)S(1)}, s32[4,1024]{1,0:T(4,128)}, u32[]{:S(2)}) copy-start(s32[4,1024]{1,0:T(4,128)} %fsrc.1) | copy-start | bytes 49156
  4.8 0.7 %copy-start.4 = (f32[4,1024]{1,0:T(4,128)S(1)}, f32[4,1024]{1,0:T(4,128)}, u32[]{:S(2)}) copy-start(f32[4,1024]{1,0:T(4,128)} %fw.1) | copy-start | bytes 49156
  5.5 0.7 %copy-start.8 = (s32[256]{0:T(256)S(1)}, s32[256]{0:T(256)}, u32[]{:S(2)}) copy-start(s32[256]{0:T(256)} %param.20) | copy-start | bytes 3076
  6.2 0.7 %copy-start.9 = (s32[256]{0:T(256)S(1)}, s32[256]{0:T(256)}, u32[]{:S(2)}) copy-start(s32[256]{0:T(256)} %param.21) | copy-start | bytes 3076
  6.9 0.7 %copy-start.10 = (f32[9]{0:T(128)S(1)}, f32[9]{0:T(128)}, u32[]{:S(2)}) copy-start(f32[9]{0:T(128)} %ld.1) | copy-start | bytes 112
  7.5 0.7 %copy-start.11 = (f32[9]{0:T(128)S(1)}, f32[9]{0:T(128)}, u32[]{:S(2)}) copy-start(f32[9]{0:T(128)} %lw.1) | copy-start | bytes 112
  8.2 0.7 %copy-start.12 = (f32[7]{0:T(128)S(1)}, f32[7]{0:T(128)}, u32[]{:S(2)}) copy-start(f32[7]{0:T(128)} %vr.1) | copy-start | bytes 88
  8.8 0.7 %copy-start.13 = (f32[7]{0:T(128)S(1)}, f32[7]{0:T(128)}, u32[]{:S(2)}) copy-start(f32[7]{0:T(128)} %cr.1) | copy-start | bytes 88

commit v2 on v1

--- a/solution.py
+++ b/solution.py
@@ -46,22 +46,23 @@
     n_atm,
     n_ocn,
     atm, ld, lw, vr, cr, skin, trig, order, ocean, nbr, fsrc, fw, ssrc, sw,
-    out_atm, out_ocean, out_surf,
+    ba0, ba1, out_ocean, out_surf,
     ld_s, lw_s, vr_s, cr_s, skin_v, trig_v, order_v, ssrc_v, sw_v,
     nb, d0, d1, coef,
-    sa0, ra0, pa0, ba0, sa1, ra1, pa1, ba1,
-    xa, xb, out_v,
-    oc_l, oc_o, oc_r, nbr_e, fsrc_e, fw_e,
+    sa0, ra0, sc0, rc0, pa0, sa1, ra1, sc1, rc1, pa1,
+    xa, xb,
+    oc_o, nbr_e, fsrc_e, fw_e,
     st, hs, mm, ff, uu, oout, sout,
     fl, fl_l, fl_r,
     local_sem, halo_send, halo_recv, oh_send, oh_recv,
-    a_send, a_recv, b_send, b_recv, self_sem, f_send, f_recv, out_sem,
+    a_send, a_recv, b_send, b_recv, c_send, c_recv, self_sem, f_send, f_recv, out_sem,
 ):
     a = lax.axis_index("atm")
     o = lax.axis_index("ocn")
     dev = a * n_ocn + o
-    up = lax.rem(a + n_atm - 1, n_atm)
-    down = lax.rem(a + 1, n_atm)
+    odd = lax.rem(a, 2)
+    mate = a + 1 - 2 * odd
+    cross = lax.rem(a + n_atm - 1 + 2 * odd, n_atm)
     total = n_atm * n_ocn
     left = lax.rem(dev + total - 1, total)
     right = lax.rem(dev + 1, total)
@@ -72,7 +73,7 @@
     fills = [
         (ld, ld_s), (lw, lw_s), (vr, vr_s), (cr, cr_s),
         (skin, skin_v), (trig, trig_v), (order, order_v), (ssrc, ssrc_v), (sw, sw_v),
-        (atm, nb.at[1]), (ocean, oc_o),
+        (atm, nb.at[0]), (ocean, oc_o),
         (nbr, nbr_e.at[:, pl.ds(256, 1024)]),
         (fsrc, fsrc_e.at[:, pl.ds(256, 1024)]),
         (fw, fw_e.at[:, pl.ds(256, 1024)]),
@@ -84,7 +85,8 @@
         copy.start()
 
     barrier = pltpu.get_barrier_semaphore()
-    partners = [(up, o), (down, o), left_id, right_id] + [(a, p) for p in peers]
+    partners = [(mate, o), left_id, right_id, (cross, o)]
+    partners += [(a, p) for p in peers] + [(cross, p) for p in peers]
     for partner in partners:
         pl.semaphore_signal(barrier, inc=1, device_id=partner, device_id_type=MESH)
     pl.semaphore_wait(barrier, len(partners))
@@ -95,27 +97,33 @@
             device_id=device, device_id_type=MESH,
         )
 
-    def halo(g):
-        f0, nf = GROUPS[g]
+    halos = []
+    for g, (f0, nf) in enumerate(GROUPS):
         rows = pl.ds(f0 * NLEV * HSUB, nf * NLEV * HSUB)
-        return [
-            remote(atm.at[rows], nb.at[0, rows], halo_send.at[g, 0], halo_recv.at[g, 0], (down, o)),
-            remote(atm.at[rows], nb.at[2, rows], halo_send.at[g, 1], halo_recv.at[g, 1], (up, o)),
-        ]
-
-    halos = [halo(0), halo(1)]
-    for copy in halos[0]:
+        copy = remote(atm.at[rows], nb.at[1, rows], halo_send.at[g], halo_recv.at[g], (mate, o))
         copy.start()
-
-    ocean3 = ocean.reshape(OLEV, 16, 128)
-    last, first = pl.ds(768, 256), pl.ds(0, 256)
-    low, high = pl.ds(0, 256), pl.ds(1280, 256)
+        halos.append(copy)
+    for copy in fills:
+        copy.wait()
+
+    unused = jnp.zeros((4, 128), F32)
+    for u in range(2, 10):
+        for f in range(2):
+            piece = oc_o[pl.ds((u - 2) * 2 + f, OLEV, stride=16), :]
+            st[pl.ds(u * OROW + f * 24, OLEV), :] = piece
+            st[pl.ds(u * OROW + f * 24 + OLEV, 4), :] = unused
+
+    def tiles(u):
+        return st.at[pl.ds(u * OROW, 2 * OROW)]
+
+    last, first = pl.ds(896, 128), pl.ds(0, 128)
+    low, high = pl.ds(128, 128), pl.ds(1280, 128)
     edge = [
-        (ocean3.at[:, pl.ds(8, 8)], oc_l.reshape(OLEV, 8, 128), right_id),
+        (tiles(8), tiles(0), right_id),
         (nbr.at[:, last], nbr_e.at[:, low], right_id),
         (fsrc.at[:, last], fsrc_e.at[:, low], right_id),
         (fw.at[:, last], fw_e.at[:, low], right_id),
-        (ocean3.at[:, pl.ds(0, 8)], oc_r.reshape(OLEV, 8, 128), left_id),
+        (tiles(2), tiles(10), left_id),
         (nbr.at[:, first], nbr_e.at[:, high], left_id),
         (fsrc.at[:, first], fsrc_e.at[:, high], left_id),
         (fw.at[:, first], fw_e.at[:, high], left_id),
@@ -126,11 +134,127 @@
     ]
     for copy in edges:
         copy.start()
-    for copy in halos[1]:
-        copy.start()
-
-    for copy in fills:
-        copy.wait()
+
+    edge_row = jnp.where(odd == 1, n_atm - 1, 0)
+    keep = jnp.where(a == edge_row, 0.0, 1.0).astype(F32)
+    sends = (sa0, sa1)
+    takes = (ra0, ra1)
+    gives = (sc0, sc1)
+    adds = (rc0, rc1)
+    packs = (pa0, pa1)
+    backs = (ba0, ba1)
+
+    def dynamics(g):
+        f0, nf = GROUPS[g]
+        n = nf * NLEV
+        sub = lax.rem(iota((n, 128), 0), NLEV)
+        diff = jnp.zeros((n, 128), F32)
+        wind = jnp.zeros((n, 128), F32)
+        for l in range(NLEV):
+            diff = jnp.where(sub == l, ld_s[l], diff)
+            wind = jnp.where(sub == l, lw_s[l], wind)
+        coef[0, pl.ds(0, n), :] = 1.0 - 4.0 * diff
+        coef[1, pl.ds(0, n), :] = diff
+        coef[2, pl.ds(0, n), :] = diff - 0.5 * wind
+        coef[3, pl.ds(0, n), :] = diff + 0.5 * wind
+        none = jnp.zeros((n, 128), F32)
+        for q in range(QS):
+            for i in range(ROWS + 1):
+                d0[i, q, pl.ds(0, n), :] = none
+                d1[i, q, pl.ds(0, n), :] = none
+            for b in range(2):
+                block = [
+                    nb[b, pl.ds(f0 * NLEV * HSUB + 4 * q + r, n, stride=HSUB), :] for r in range(ROWS)
+                ]
+                for r in range(ROWS):
+                    piece = jnp.where(odd == 1, block[ROWS - 1 - r], block[r])
+                    d0[1 + (b + 1) * ROWS + r, q, pl.ds(0, n), :] = piece
+        lane = iota((n, 128), 1)
+        bufs = (d0, d1)
+
+        def update(src, i):
+            here = [src[i, q, pl.ds(0, n), :] for q in range(QS)]
+            to_east = [pltpu.roll(x, 1, 1) for x in here]
+            to_west = [pltpu.roll(x, 127, 1) for x in here]
+            new = []
+            for q in range(QS):
+                west = jnp.where(lane == 0, to_east[(q - 1) % QS], to_east[q])
+                east = jnp.where(lane == 127, to_west[(q + 1) % QS], to_west[q])
+                beside = src[i - 1, q, pl.ds(0, n), :] + src[i + 1, q, pl.ds(0, n), :]
+                new.append(
+                    coef[0, pl.ds(0, n), :] * here[q]
+                    + coef[1, pl.ds(0, n), :] * beside
+                    + coef[2, pl.ds(0, n), :] * east
+                    + coef[3, pl.ds(0, n), :] * west
+                )
+            return new
+
+        for step in range(1, DYN_STEPS):
+            src, dst = bufs[(step - 1) % 2], bufs[step % 2]
+
+            def row(i, carry):
+                scale = jnp.where(i <= ROWS, keep, 1.0)
+                for q, value in enumerate(update(src, i)):
+                    dst[i, q, pl.ds(0, n), :] = value * scale
+                return carry
+
+            lax.fori_loop(1 + ROWS - step, 1 + 3 * ROWS - step, row, 0)
+
+        src = bufs[(DYN_STEPS - 1) % 2]
+
+        def last_row(dst, scale):
+            def body(i, carry):
+                r = jnp.where(odd == 1, ROWS - 1 - i, i)
+                first = 1 if dst is gives[g] else 1 + ROWS
+                for q, value in enumerate(update(src, i + first)):
+                    if scale is not None:
+                        value = value * scale
+                    dst[r * 2 + q // 2, pl.ds((q % 2) * n, n), :] = value
+                return carry
+
+            return body
+
+        lax.fori_loop(0, ROWS, last_row(gives[g], keep), 0)
+        everyone = [o] + peers
+        copies = [
+            remote(gives[g].at[p], adds[g].at[o], c_send.at[g, p], c_recv.at[g, o], (cross, p))
+            for p in everyone
+        ]
+        for copy in copies:
+            copy.start()
+        arrivals = [
+            remote(gives[g].at[p], adds[g].at[p], c_send.at[g, p], c_recv.at[g, p], (cross, p))
+            for p in everyone
+        ]
+        lax.fori_loop(0, ROWS, last_row(sends[g], None), 0)
+        return copies, None, arrivals
+
+    def exchange(src, dst, send, recv, own_sem, g):
+        copies = [
+            remote(src.at[p], dst.at[o], send.at[g, p], recv.at[g, o], (a, p)) for p in peers
+        ]
+        own = pltpu.make_async_copy(src.at[o], dst.at[o], own_sem)
+        for copy in copies:
+            copy.start()
+        own.start()
+        arrivals = [
+            remote(src.at[p], dst.at[p], send.at[g, p], recv.at[g, p], (a, p)) for p in peers
+        ]
+        return copies, own, arrivals
+
+    def landed(handle):
+        copies, own, arrivals = handle
+        if own is not None:
+            own.wait()
+        for copy in arrivals:
+            copy.wait_recv()
+
+    out_there = []
+    out_cross = []
+    for g in range(2):
+        halos[g].wait_recv()
+        out_cross.append(dynamics(g))
+        out_there.append(exchange(sends[g], takes[g], a_send, a_recv, self_sem.at[g], g))
 
     hit = jnp.where(trig_v[...] > 0, order_v[...], -1).astype(F32)
     hit = jnp.concatenate([hit, jnp.full((6, 128), -1.0, F32)], axis=0)
@@ -144,18 +268,8 @@
 
     for copy in edges:
         copy.wait_recv()
-
-    unused = jnp.zeros((4, 128), F32)
-    for u in range(NT):
-        for f in range(2):
-            if u < 2:
-                piece = oc_l[pl.ds((u + 2) * 2 + f, OLEV, stride=8), :]
-            elif u < 10:
-                piece = oc_o[pl.ds((u - 2) * 2 + f, OLEV, stride=16), :]
-            else:
-                piece = oc_r[pl.ds((u - 10) * 2 + f, OLEV, stride=8), :]
-            st[pl.ds(u * OROW + f * 24, OLEV), :] = piece
-            st[pl.ds(u * OROW + f * 24 + OLEV, 4), :] = unused
+    for copy in edges:
+        copy.wait_send()
 
     def build(u, carry):
         at = pl.multiple_of(u * 128, 128)
@@ -206,89 +320,6 @@
 
     spread(False)
 
-    keep_up = jnp.where(a > 0, 1.0, 0.0).astype(F32)
-    keep_down = jnp.where(a < n_atm - 1, 1.0, 0.0).astype(F32)
-    sends = (sa0, sa1)
-    takes = (ra0, ra1)
-    packs = (pa0, pa1)
-    backs = (ba0, ba1)
-
-    def dynamics(g):
-        f0, nf = GROUPS[g]
-        n = nf * NLEV
-        sub = lax.rem(iota((n, 128), 0), NLEV)
-        diff = jnp.zeros((n, 128), F32)
-        wind = jnp.zeros((n, 128), F32)
-        for l in range(NLEV):
-            diff = jnp.where(sub == l, ld_s[l], diff)
-            wind = jnp.where(sub == l, lw_s[l], wind)
-        coef[0, pl.ds(0, n), :] = 1.0 - 4.0 * diff
-        coef[1, pl.ds(0, n), :] = diff
-        coef[2, pl.ds(0, n), :] = diff - 0.5 * wind
-        coef[3, pl.ds(0, n), :] = diff + 0.5 * wind
-        for b in range(3):
-            for r in range(ROWS):
-                for q in range(QS):
-                    piece = nb[b, pl.ds(f0 * NLEV * HSUB + 4 * q + r, n, stride=HSUB), :]
-                    if b == 0:
-                        piece = piece * keep_up
-                    if b == 2:
-                        piece = piece * keep_down
-                    d0[b * ROWS + r, q, pl.ds(0, n), :] = piece
-        lane = iota((n, 128), 1)
-        bufs = (d0, d1)
-        for step in range(1, DYN_STEPS + 1):
-            src, dst = bufs[(step - 1) % 2], bufs[step % 2]
-
-            def row(i, carry):
-                here = [src[i, q, pl.ds(0, n), :] for q in range(QS)]
-                to_east = [pltpu.roll(x, 1, 1) for x in here]
-                to_west = [pltpu.roll(x, 127, 1) for x in here]
-                for q in range(QS):
-                    west = jnp.where(lane == 0, to_east[(q - 1) % QS], to_east[q])
-                    east = jnp.where(lane == 127, to_west[(q + 1) % QS], to_west[q])
-                    beside = src[i - 1, q, pl.ds(0, n), :] + src[i + 1, q, pl.ds(0, n), :]
-                    new = (
-                        coef[0, pl.ds(0, n), :] * here[q]
-                        + coef[1, pl.ds(0, n), :] * beside
-                        + coef[2, pl.ds(0, n), :] * east
-                        + coef[3, pl.ds(0, n), :] * west
-                    )
-                    if step == DYN_STEPS:
-                        sends[g][(i - ROWS) * 2 + q // 2, pl.ds((q % 2) * n, n), :] = new
-                    else:
-                        keep = jnp.where(i < ROWS, keep_up, jnp.where(i >= 2 * ROWS, keep_down, 1.0))
-                        dst[i, q, pl.ds(0, n), :] = new * keep
-                return carry
-
-            lax.fori_loop(step, 3 * ROWS - step, row, 0)
-
-    def exchange(src, dst, send, recv, g):
-        copies = [
-            remote(src.at[p], dst.at[o], send.at[g, p], recv.at[g, o], (a, p)) for p in peers
-        ]
-        own = pltpu.make_async_copy(src.at[o], dst.at[o], self_sem.at[g])
-        for copy in copies:
-            copy.start()
-        own.start()
-        arrivals = [
-            remote(src.at[p], dst.at[p], send.at[g, p], recv.at[g, p], (a, p)) for p in peers
-        ]
-        return copies, own, arrivals
-
-    def landed(handle):
-        copies, own, arrivals = handle
-        own.wait()
-        for copy in arrivals:
-            copy.wait_recv()
-
-    out_there = []
-    for g in range(2):
-        for copy in halos[g]:
-            copy.wait_recv()
-        dynamics(g)
-        out_there.append(exchange(sends[g], takes[g], a_send, a_recv, g))
-
     def physics(g):
         f0, nf = GROUPS[g]
         n = 2 * nf
@@ -303,7 +334,8 @@
         rate = rate * jnp.where(sub < nf, active[0], active[1])
 
         for lev in range(LEV):
-            x[lev, pl.ds(0, n), :] = takes[g][lev // NLEV, pl.ds(lev % NLEV, n, stride=NLEV), :]
+            rows = pl.ds(lev % NLEV, n, stride=NLEV)
+            x[lev, pl.ds(0, n), :] = takes[g][lev // NLEV, rows, :] + adds[g][lev // NLEV, rows, :]
 
         def vertical(i, carry):
             here = x[0, pl.ds(0, n), :]
@@ -337,6 +369,7 @@
             packs[g][lev // NLEV, pl.ds(lev % NLEV, n, stride=NLEV), :] = x[lev, pl.ds(0, n), :]
 
     landed(out_there[0])
+    landed(out_cross[0])
     physics(0)
 
     fl[...] = jnp.zeros((8, 128), F32)
@@ -356,11 +389,12 @@
     for copy in fluxes:
         copy.start()
     pack(0)
-    back_home = [exchange(packs[0], backs[0], b_send, b_recv, 0)]
+    back_home = [exchange(packs[0], backs[0], b_send, b_recv, self_sem.at[2], 0)]
     landed(out_there[1])
+    landed(out_cross[1])
     physics(1)
     pack(1)
-    back_home.append(exchange(packs[1], backs[1], b_send, b_recv, 1))
+    back_home.append(exchange(packs[1], backs[1], b_send, b_recv, self_sem.at[3], 1))
 
     for copy in fluxes:
         copy.wait_recv()
@@ -421,26 +455,38 @@
     surf_copy = pltpu.make_async_copy(sout, out_surf, out_sem.at[1])
     surf_copy.start()
 
-    out_copies = [ocean_copy, surf_copy]
-    for g in range(2):
-        f0, nf = GROUPS[g]
+    for handle in back_home:
+        landed(handle)
+    for copy in halos + fluxes:
+        copy.wait_send()
+    for copies, own, arrivals in out_there + out_cross + back_home:
+        for copy in copies:
+            copy.wait_send()
+    ocean_copy.wait()
+    surf_copy.wait()
+
+
+def finish(ba0, ba1, ocean, surf, out_atm, out_ocean, out_surf, b0, b1, ocean_v, surf_v, out_v, sem):
+    ins = ((ba0, b0), (ba1, b1), (ocean, ocean_v), (surf, surf_v))
+    copies = [pltpu.make_async_copy(src, dst, sem.at[i]) for i, (src, dst) in enumerate(ins)]
+    for copy in copies:
+        copy.start()
+    outs = []
+    for g, (f0, nf) in enumerate(GROUPS):
         n = nf * NLEV
-        landed(back_home[g])
+        copies[g].wait()
         for r in range(ROWS):
             for q in range(QS):
-                piece = backs[g][2 * r + q // 2, pl.ds((q % 2) * n, n), :]
+                piece = (b0, b1)[g][2 * r + q // 2, pl.ds((q % 2) * n, n), :]
                 out_v[pl.ds(f0 * NLEV * HSUB + 4 * q + r, n, stride=HSUB), :] = piece
         rows = pl.ds(f0 * NLEV * HSUB, n * HSUB)
-        copy = pltpu.make_async_copy(out_v.at[rows], out_atm.at[rows], out_sem.at[2 + g])
-        copy.start()
-        out_copies.append(copy)
-
-    for copy in halos[0] + halos[1] + edges + fluxes:
-        copy.wait_send()
-    for copies, own, arrivals in out_there + back_home:
-        for copy in copies:
-            copy.wait_send()
-    for copy in out_copies:
+        outs.append(pltpu.make_async_copy(out_v.at[rows], out_atm.at[rows], sem.at[4 + g]))
+        outs[-1].start()
+    for i, (src, dst) in enumerate(((ocean_v, out_ocean), (surf_v, out_surf))):
+        copies[2 + i].wait()
+        outs.append(pltpu.make_async_copy(src, dst, sem.at[6 + i]))
+        outs[-1].start()
+    for copy in outs:
         copy.wait()
 
 
@@ -455,42 +501,56 @@
     def vmem(*shape, dtype=F32):
         return pltpu.VMEM(shape, dtype)
 
-    new_atm, new_ocean, surf = pl.pallas_call(
+    parts = pl.pallas_call(
         functools.partial(kernel, n_atm, n_ocn),
         out_shape=(
-            jax.ShapeDtypeStruct((1008, 128), F32),
+            jax.ShapeDtypeStruct((8, 72, 128), F32),
+            jax.ShapeDtypeStruct((8, 56, 128), F32),
             jax.ShapeDtypeStruct((320, 128), F32),
             jax.ShapeDtypeStruct((2, 128), F32),
         ),
         in_specs=[hbm] * 14,
-        out_specs=(hbm,) * 3,
+        out_specs=(hbm,) * 4,
         scratch_shapes=[
             pltpu.SMEM((NLEV,), F32), pltpu.SMEM((NLEV,), F32),
             pltpu.SMEM((FIELDS,), F32), pltpu.SMEM((FIELDS,), F32),
             vmem(2, 128), vmem(2, 128, dtype=jnp.int32), vmem(2, 128, dtype=jnp.int32),
             vmem(4, 256, dtype=jnp.int32), vmem(4, 256),
-            vmem(3, 1008, 128), vmem(12, QS, 40, 128), vmem(12, QS, 40, 128), vmem(4, 40, 128),
-            vmem(8, 72, 128), vmem(8, 72, 128), vmem(8, 72, 128), vmem(8, 72, 128),
-            vmem(8, 56, 128), vmem(8, 56, 128), vmem(8, 56, 128), vmem(8, 56, 128),
-            vmem(LEV, 8, 128), vmem(LEV, 8, 128), vmem(1008, 128),
-            vmem(160, 128), vmem(320, 128), vmem(160, 128),
+            vmem(2, 1008, 128), vmem(13, QS, 40, 128), vmem(13, QS, 40, 128), vmem(4, 40, 128),
+            *[vmem(8, 72, 128)] * 5, *[vmem(8, 56, 128)] * 5,
+            vmem(LEV, 8, 128), vmem(LEV, 8, 128),
+            vmem(320, 128),
             vmem(NBR, 1536, dtype=jnp.int32), vmem(NW, 1536, dtype=jnp.int32), vmem(NW, 1536),
             vmem(NT * OROW, 128), vmem(NT, PARTS * OROW, 128, dtype=BF16),
             vmem(NT - 2, 384, 128, dtype=BF16), vmem(NT * OROW, 128), vmem(16, 128),
             vmem(320, 128), vmem(2, 128),
             vmem(8, 128), vmem(8, 128), vmem(8, 128),
-            dma((14,)), dma((2, 2)), dma((2, 2)), dma((8,)), dma((8,)),
-            dma((2, 8)), dma((2, 8)), dma((2, 8)), dma((2, 8)), dma((2,)),
-            dma((2,)), dma((2,)), dma((4,)),
+            dma((14,)), dma((2,)), dma((2,)), dma((8,)), dma((8,)),
+            dma((2, 8)), dma((2, 8)), dma((2, 8)), dma((2, 8)), dma((2, 8)), dma((2, 8)), dma((4,)),
+            dma((2,)), dma((2,)), dma((2,)),
         ],
         compiler_params=pltpu.CompilerParams(
-            collective_id=0, has_side_effects=True, vmem_limit_bytes=40 * 1024 * 1024
+            collective_id=0, has_side_effects=True, vmem_limit_bytes=60 * 1024 * 1024
         ),
     )(
         atm, level_diffusion, level_wind, vertical_rate, convective_rate,
         ocean_skin.reshape(2, 128), trigger.reshape(2, 128), group_order.reshape(2, 128),
         ocean, ocean_neighbors, flux_sources, flux_weights, surface_sources, surface_weights,
     )
+    new_atm, new_ocean, surf = pl.pallas_call(
+        finish,
+        out_shape=(
+            jax.ShapeDtypeStruct((1008, 128), F32),
+            jax.ShapeDtypeStruct((320, 128), F32),
+            jax.ShapeDtypeStruct((2, 128), F32),
+        ),
+        in_specs=[hbm] * 4,
+        out_specs=(hbm,) * 3,
+        scratch_shapes=[
+            vmem(8, 72, 128), vmem(8, 56, 128), vmem(320, 128), vmem(2, 128), vmem(1008, 128), dma((8,)),
+        ],
+        compiler_params=pltpu.CompilerParams(vmem_limit_bytes=60 * 1024 * 1024),
+    )(*parts)
     new_atm = new_atm.reshape(FIELDS, NLEV, QS, ROWS, 128).transpose(0, 1, 3, 2, 4)
     new_ocean = new_ocean.reshape(OLEV, 8, 2, 128).transpose(0, 2, 1, 3).reshape(OLEV, 2, 1024)
     return (

time: 58.7 us -> 44.4 us (0.76)
  the two profiles are of different devices: /device:TPU:16 before, /device:TPU:3 now
where the time goes in v2:
time: 44.4 us; the launch traced here: 44.3 us
  Pallas kernels  43.7 us (98%)
  between operations  0.64 us (1%)
    pallas_call x1, Pallas kernels, local(): pl.pallas_call(functools.partial(kernel, n_atm, n_ocn), out_shape=(jax.Sh...  41.7 us
    pallas_call x1, Pallas kernels, local(): pl.pallas_call(finish, out_shape=(jax.ShapeDtypeStruct((1008, 128), F32),...  2 us

profile of v2, /device:TPU:3, one launch (start us, length us, event | category | flops | bytes accessed | tf_op | source)
XLA Modules:
  0.0 44.3 jit_solution(5666314589169874433)
XLA Ops:
  0.6 41.7 %shard_map.157 = (f32[8,72,128]{2,1,0:T(8,128)}, f32[8,56,128]{2,1,0:T(8,128)}, f32[320,128]{1,0:T(8,128)}, f32[2,128]{1,0:T(2,128)}) custom-call(f32[1008,128]{1,0:T(8,128)} %bitcast.28, f32[9]{0:T(128)} %ld.1, f32[9]{0:T(128)} %lw.1, f32[7]{0:T(128)} %vr.1, f32[7]{0:T(128)} %cr.1, f32[2,128]{1,0:T(2,128)} %bitcast.30, s32[2,128]{1,0:T(2,128)} %bitcast.31, ...), custom_call_target="tpu_custom_call" | custom-call | tf_op jit(solution)/shard_map/pallas_call | solution.py:504
  42.3 2.0 %shard_map.158 = (f32[1008,128]{1,0:T(8,128)}, f32[320,128]{1,0:T(8,128)}, f32[2,128]{1,0:T(2,128)}) custom-call(f32[8,72,128]{2,1,0:T(8,128)} %get-tuple-element.10.ba0, f32[8,56,128]{2,1,0:T(8,128)} %get-tuple-element.11.ba1, f32[320,128]{1,0:T(8,128)} %get-tuple-element.12.ocean, f32[2,128]{1,0:T(2,128)} %get-tuple-element.13.surf), custom_call_target="tpu_custom_call" | custom-call | tf_op jit(solution)/shard_map/pallas_call | solution.py:540

commit v3 on v2

--- a/solution.py
+++ b/solution.py
@@ -198,7 +198,7 @@
                     dst[i, q, pl.ds(0, n), :] = value * scale
                 return carry
 
-            lax.fori_loop(1 + ROWS - step, 1 + 3 * ROWS - step, row, 0)
+            lax.fori_loop(1 + ROWS - step, 1 + 3 * ROWS - step, row, 0, unroll=True)
 
         src = bufs[(DYN_STEPS - 1) % 2]
 
@@ -214,7 +214,7 @@
 
             return body
 
-        lax.fori_loop(0, ROWS, last_row(gives[g], keep), 0)
+        lax.fori_loop(0, ROWS, last_row(gives[g], keep), 0, unroll=True)
         everyone = [o] + peers
         copies = [
             remote(gives[g].at[p], adds[g].at[o], c_send.at[g, p], c_recv.at[g, o], (cross, p))
@@ -226,7 +226,7 @@
             remote(gives[g].at[p], adds[g].at[p], c_send.at[g, p], c_recv.at[g, p], (cross, p))
             for p in everyone
         ]
-        lax.fori_loop(0, ROWS, last_row(sends[g], None), 0)
+        lax.fori_loop(0, ROWS, last_row(sends[g], None), 0, unroll=True)
         return copies, None, arrivals
 
     def exchange(src, dst, send, recv, own_sem, g):
@@ -284,7 +284,7 @@
         mm[u - 1, pl.ds(288, 96), :] = jnp.zeros((96, 128), BF16)
         return carry
 
-    lax.fori_loop(1, NT - 1, build, 0)
+    lax.fori_loop(1, NT - 1, build, 0, unroll=True)
 
     level_row = lax.rem(iota((OROW, 128), 0), 24)
 
@@ -297,7 +297,7 @@
                 rest = rest - piece.astype(F32)
             return carry
 
-        lax.fori_loop(0, NT, split, 0)
+        lax.fori_loop(0, NT, split, 0, unroll=True)
 
         def tile(u, carry):
             source = jnp.concatenate([hs[u - 1], hs[u], hs[u + 1]], axis=1)
@@ -316,7 +316,7 @@
             st[rows, :] = jnp.where(level_row < OLEV, here, 0.0)
             return carry
 
-        lax.fori_loop(1, NT - 1, tile, 0)
+        lax.fori_loop(1, NT - 1, tile, 0, unroll=True)
 
     spread(False)
 

time: 44.4 us -> 39.1 us (0.88)
  the two profiles are of different devices: /device:TPU:3 before, /device:TPU:1 now
where the time goes in v3:
time: 39.1 us; the launch traced here: 39 us
  Pallas kernels  38.3 us (98%)
  between operations  0.64 us (2%)
    pallas_call x1, Pallas kernels, local(): pl.pallas_call(functools.partial(kernel, n_atm, n_ocn), out_shape=(jax.Sh...  36.3 us
    pallas_call x1, Pallas kernels, local(): pl.pallas_call(finish, out_shape=(jax.ShapeDtypeStruct((1008, 128), F32),...  2 us

profile of v3, /device:TPU:1, one launch (start us, length us, event | category | flops | bytes accessed | tf_op | source)
XLA Modules:
  0.0 39.0 jit_solution(10727378955564834483)
XLA Ops:
  0.6 36.3 %shard_map.157 = (f32[8,72,128]{2,1,0:T(8,128)}, f32[8,56,128]{2,1,0:T(8,128)}, f32[320,128]{1,0:T(8,128)}, f32[2,128]{1,0:T(2,128)}) custom-call(f32[1008,128]{1,0:T(8,128)} %bitcast.28, f32[9]{0:T(128)} %ld.1, f32[9]{0:T(128)} %lw.1, f32[7]{0:T(128)} %vr.1, f32[7]{0:T(128)} %cr.1, f32[2,128]{1,0:T(2,128)} %bitcast.30, s32[2,128]{1,0:T(2,128)} %bitcast.31, ...), custom_call_target="tpu_custom_call" | custom-call | tf_op jit(solution)/shard_map/pallas_call | solution.py:504
  37.0 2.0 %shard_map.158 = (f32[1008,128]{1,0:T(8,128)}, f32[320,128]{1,0:T(8,128)}, f32[2,128]{1,0:T(2,128)}) custom-call(f32[8,72,128]{2,1,0:T(8,128)} %get-tuple-element.10.ba0, f32[8,56,128]{2,1,0:T(8,128)} %get-tuple-element.11.ba1, f32[320,128]{1,0:T(8,128)} %get-tuple-element.12.ocean, f32[2,128]{1,0:T(2,128)} %get-tuple-element.13.surf), custom_call_target="tpu_custom_call" | custom-call | tf_op jit(solution)/shard_map/pallas_call | solution.py:540

commit v4 on v3

--- a/solution.py
+++ b/solution.py
@@ -48,7 +48,7 @@
     atm, ld, lw, vr, cr, skin, trig, order, ocean, nbr, fsrc, fw, ssrc, sw,
     ba0, ba1, out_ocean, out_surf,
     ld_s, lw_s, vr_s, cr_s, skin_v, trig_v, order_v, ssrc_v, sw_v,
-    nb, d0, d1, coef,
+    nb, dd, coef,
     sa0, ra0, sc0, rc0, pa0, sa1, ra1, sc1, rc1, pa1,
     xa, xb,
     oc_o, nbr_e, fsrc_e, fw_e,
@@ -68,7 +68,11 @@
     right = lax.rem(dev + 1, total)
     left_id = (left // n_ocn, lax.rem(left, n_ocn))
     right_id = (right // n_ocn, lax.rem(right, n_ocn))
-    peers = [lax.rem(o + d, n_ocn) for d in range(1, n_ocn)]
+    def at_offset(dx, dy):
+        return lax.rem(o // 2 + dx, n_ocn // 2) * 2 + lax.rem(o + dy, 2)
+
+    peers = [at_offset(*d) for d in ((2, 1), (1, 1), (3, 1), (2, 0), (1, 0), (3, 0), (0, 1))]
+    others = [at_offset(*d) for d in ((2, 0), (1, 0), (3, 0), (2, 1), (0, 0), (1, 1), (3, 1), (0, 1))]
 
     fills = [
         (ld, ld_s), (lw, lw_s), (vr, vr_s), (cr, cr_s),
@@ -84,18 +88,143 @@
     for copy in fills:
         copy.start()
 
+    edge_row = jnp.where(odd == 1, n_atm - 1, 0)
+    inside = a != edge_row
+    keep = jnp.where(inside, 1.0, 0.0).astype(F32)
     barrier = pltpu.get_barrier_semaphore()
-    partners = [(mate, o), left_id, right_id, (cross, o)]
-    partners += [(a, p) for p in peers] + [(cross, p) for p in peers]
-    for partner in partners:
-        pl.semaphore_signal(barrier, inc=1, device_id=partner, device_id_type=MESH)
-    pl.semaphore_wait(barrier, len(partners))
+    partners = [(mate, o), left_id, right_id] + [(a, p) for p in peers]
+
+    def greet(devices):
+        for device in devices:
+            pl.semaphore_signal(barrier, inc=1, device_id=device, device_id_type=MESH)
+
+    greet(partners)
+
+    @pl.when(inside)
+    def _():
+        greet([(cross, p) for p in others])
 
     def remote(src, dst, send, recv, device):
         return pltpu.make_async_remote_copy(
             src_ref=src, dst_ref=dst, send_sem=send, recv_sem=recv,
             device_id=device, device_id_type=MESH,
         )
+
+    for copy in fills:
+        copy.wait()
+
+    sends = (sa0, sa1)
+    takes = (ra0, ra1)
+    gives = (sc0, sc1)
+    adds = (rc0, rc1)
+    packs = (pa0, pa1)
+    backs = (ba0, ba1)
+
+    def enter(g, b):
+        f0, nf = GROUPS[g]
+        n = nf * NLEV
+        for q in range(QS):
+            block = [
+                nb[b, pl.ds(f0 * NLEV * HSUB + 4 * q + r, n, stride=HSUB), :] for r in range(ROWS)
+            ]
+            for r in range(ROWS):
+                piece = jnp.where(odd == 1, block[ROWS - 1 - r], block[r])
+                dd[g, 0, 1 + (b + 1) * ROWS + r, q, pl.ds(0, n), :] = piece
+
+    def update(g, step, i):
+        n = GROUPS[g][1] * NLEV
+        rows = pl.ds(0, n)
+        lane = iota((n, 128), 1)
+        here = [dd[g, step - 1, i, q, rows, :] for q in range(QS)]
+        to_east = [pltpu.roll(x, 1, 1) for x in here]
+        to_west = [pltpu.roll(x, 127, 1) for x in here]
+        new = []
+        for q in range(QS):
+            west = jnp.where(lane == 0, to_east[(q - 1) % QS], to_east[q])
+            east = jnp.where(lane == 127, to_west[(q + 1) % QS], to_west[q])
+            beside = dd[g, step - 1, i - 1, q, rows, :] + dd[g, step - 1, i + 1, q, rows, :]
+            new.append(
+                coef[g, 0, rows, :] * here[q]
+                + coef[g, 1, rows, :] * beside
+                + coef[g, 2, rows, :] * east
+                + coef[g, 3, rows, :] * west
+            )
+        return new
+
+    def steps(g, first, dst):
+        n = GROUPS[g][1] * NLEV
+
+        def scaled(i, value):
+            return value * jnp.where(i <= ROWS, keep, 1.0) if first <= ROWS else value
+
+        for step in range(1, DYN_STEPS):
+
+            def row(i, carry):
+                for q, value in enumerate(update(g, step, i)):
+                    dd[g, step, i, q, pl.ds(0, n), :] = scaled(i, value)
+                return carry
+
+            begin = first + DYN_STEPS - step
+            lax.fori_loop(begin, begin + ROWS, row, 0, unroll=True)
+
+        def last(i, carry):
+            r = jnp.where(odd == 1, ROWS - 1 - i, i)
+            for q, value in enumerate(update(g, DYN_STEPS, i + first)):
+                dst[r * 2 + q // 2, pl.ds((q % 2) * n, n), :] = scaled(i + first, value)
+            return carry
+
+        lax.fori_loop(0, ROWS, last, 0, unroll=True)
+
+    def contribute(g):
+        n = GROUPS[g][1] * NLEV
+        sub = lax.rem(iota((n, 128), 0), NLEV)
+        diff = jnp.zeros((n, 128), F32)
+        wind = jnp.zeros((n, 128), F32)
+        for l in range(NLEV):
+            diff = jnp.where(sub == l, ld_s[l], diff)
+            wind = jnp.where(sub == l, lw_s[l], wind)
+        coef[g, 0, pl.ds(0, n), :] = 1.0 - 4.0 * diff
+        coef[g, 1, pl.ds(0, n), :] = diff
+        coef[g, 2, pl.ds(0, n), :] = diff - 0.5 * wind
+        coef[g, 3, pl.ds(0, n), :] = diff + 0.5 * wind
+        none = jnp.zeros((n, 128), F32)
+        for step in range(DYN_STEPS):
+            for q in range(QS):
+                for i in (ROWS - 1 - step, ROWS - step):
+                    dd[g, step, i, q, pl.ds(0, n), :] = none
+        enter(g, 0)
+        steps(g, 1, gives[g])
+
+    def send_across(g):
+        copies = [
+            remote(gives[g].at[p], adds[g].at[o], c_send.at[g, p], c_recv.at[g, o], (cross, p))
+            for p in others
+        ]
+        arrivals = [
+            remote(gives[g].at[p], adds[g].at[p], c_send.at[g, p], c_recv.at[g, p], (cross, p))
+            for p in others
+        ]
+
+        @pl.when(inside)
+        def _():
+            for copy in copies:
+                copy.start()
+
+        @pl.when(jnp.logical_not(inside))
+        def _():
+            adds[g][...] = jnp.zeros(adds[g].shape, F32)
+
+        return copies, arrivals
+
+    contribute(0)
+
+    @pl.when(inside)
+    def _():
+        pl.semaphore_wait(barrier, len(partners) + len(others))
+
+    @pl.when(jnp.logical_not(inside))
+    def _():
+        pl.semaphore_wait(barrier, len(partners))
 
     halos = []
     for g, (f0, nf) in enumerate(GROUPS):
@@ -103,8 +232,6 @@
         copy = remote(atm.at[rows], nb.at[1, rows], halo_send.at[g], halo_recv.at[g], (mate, o))
         copy.start()
         halos.append(copy)
-    for copy in fills:
-        copy.wait()
 
     unused = jnp.zeros((4, 128), F32)
     for u in range(2, 10):
@@ -135,99 +262,7 @@
     for copy in edges:
         copy.start()
 
-    edge_row = jnp.where(odd == 1, n_atm - 1, 0)
-    keep = jnp.where(a == edge_row, 0.0, 1.0).astype(F32)
-    sends = (sa0, sa1)
-    takes = (ra0, ra1)
-    gives = (sc0, sc1)
-    adds = (rc0, rc1)
-    packs = (pa0, pa1)
-    backs = (ba0, ba1)
-
-    def dynamics(g):
-        f0, nf = GROUPS[g]
-        n = nf * NLEV
-        sub = lax.rem(iota((n, 128), 0), NLEV)
-        diff = jnp.zeros((n, 128), F32)
-        wind = jnp.zeros((n, 128), F32)
-        for l in range(NLEV):
-            diff = jnp.where(sub == l, ld_s[l], diff)
-            wind = jnp.where(sub == l, lw_s[l], wind)
-        coef[0, pl.ds(0, n), :] = 1.0 - 4.0 * diff
-        coef[1, pl.ds(0, n), :] = diff
-        coef[2, pl.ds(0, n), :] = diff - 0.5 * wind
-        coef[3, pl.ds(0, n), :] = diff + 0.5 * wind
-        none = jnp.zeros((n, 128), F32)
-        for q in range(QS):
-            for i in range(ROWS + 1):
-                d0[i, q, pl.ds(0, n), :] = none
-                d1[i, q, pl.ds(0, n), :] = none
-            for b in range(2):
-                block = [
-                    nb[b, pl.ds(f0 * NLEV * HSUB + 4 * q + r, n, stride=HSUB), :] for r in range(ROWS)
-                ]
-                for r in range(ROWS):
-                    piece = jnp.where(odd == 1, block[ROWS - 1 - r], block[r])
-                    d0[1 + (b + 1) * ROWS + r, q, pl.ds(0, n), :] = piece
-        lane = iota((n, 128), 1)
-        bufs = (d0, d1)
-
-        def update(src, i):
-            here = [src[i, q, pl.ds(0, n), :] for q in range(QS)]
-            to_east = [pltpu.roll(x, 1, 1) for x in here]
-            to_west = [pltpu.roll(x, 127, 1) for x in here]
-            new = []
-            for q in range(QS):
-                west = jnp.where(lane == 0, to_east[(q - 1) % QS], to_east[q])
-                east = jnp.where(lane == 127, to_west[(q + 1) % QS], to_west[q])
-                beside = src[i - 1, q, pl.ds(0, n), :] + src[i + 1, q, pl.ds(0, n), :]
-                new.append(
-                    coef[0, pl.ds(0, n), :] * here[q]
-                    + coef[1, pl.ds(0, n), :] * beside
-                    + coef[2, pl.ds(0, n), :] * east
-                    + coef[3, pl.ds(0, n), :] * west
-                )
-            return new
-
-        for step in range(1, DYN_STEPS):
-            src, dst = bufs[(step - 1) % 2], bufs[step % 2]
-
-            def row(i, carry):
-                scale = jnp.where(i <= ROWS, keep, 1.0)
-                for q, value in enumerate(update(src, i)):
-                    dst[i, q, pl.ds(0, n), :] = value * scale
-                return carry
-
-            lax.fori_loop(1 + ROWS - step, 1 + 3 * ROWS - step, row, 0, unroll=True)
-
-        src = bufs[(DYN_STEPS - 1) % 2]
-
-        def last_row(dst, scale):
-            def body(i, carry):
-                r = jnp.where(odd == 1, ROWS - 1 - i, i)
-                first = 1 if dst is gives[g] else 1 + ROWS
-                for q, value in enumerate(update(src, i + first)):
-                    if scale is not None:
-                        value = value * scale
-                    dst[r * 2 + q // 2, pl.ds((q % 2) * n, n), :] = value
-                return carry
-
-            return body
-
-        lax.fori_loop(0, ROWS, last_row(gives[g], keep), 0, unroll=True)
-        everyone = [o] + peers
-        copies = [
-            remote(gives[g].at[p], adds[g].at[o], c_send.at[g, p], c_recv.at[g, o], (cross, p))
-            for p in everyone
-        ]
-        for copy in copies:
-            copy.start()
-        arrivals = [
-            remote(gives[g].at[p], adds[g].at[p], c_send.at[g, p], c_recv.at[g, p], (cross, p))
-            for p in everyone
-        ]
-        lax.fori_loop(0, ROWS, last_row(sends[g], None), 0, unroll=True)
-        return copies, None, arrivals
+    out_cross = [send_across(0)]
 
     def exchange(src, dst, send, recv, own_sem, g):
         copies = [
@@ -242,19 +277,27 @@
         ]
         return copies, own, arrivals
 
+    def crossed(handle):
+        @pl.when(inside)
+        def _():
+            for copy in handle[1]:
+                copy.wait_recv()
+
     def landed(handle):
         copies, own, arrivals = handle
-        if own is not None:
-            own.wait()
+        own.wait()
         for copy in arrivals:
             copy.wait_recv()
 
     out_there = []
-    out_cross = []
     for g in range(2):
         halos[g].wait_recv()
-        out_cross.append(dynamics(g))
+        enter(g, 1)
+        steps(g, 1 + ROWS, sends[g])
         out_there.append(exchange(sends[g], takes[g], a_send, a_recv, self_sem.at[g], g))
+        if g == 0:
+            contribute(1)
+            out_cross.append(send_across(1))
 
     hit = jnp.where(trig_v[...] > 0, order_v[...], -1).astype(F32)
     hit = jnp.concatenate([hit, jnp.full((6, 128), -1.0, F32)], axis=0)
@@ -369,7 +412,7 @@
             packs[g][lev // NLEV, pl.ds(lev % NLEV, n, stride=NLEV), :] = x[lev, pl.ds(0, n), :]
 
     landed(out_there[0])
-    landed(out_cross[0])
+    crossed(out_cross[0])
     physics(0)
 
     fl[...] = jnp.zeros((8, 128), F32)
@@ -391,7 +434,7 @@
     pack(0)
     back_home = [exchange(packs[0], backs[0], b_send, b_recv, self_sem.at[2], 0)]
     landed(out_there[1])
-    landed(out_cross[1])
+    crossed(out_cross[1])
     physics(1)
     pack(1)
     back_home.append(exchange(packs[1], backs[1], b_send, b_recv, self_sem.at[3], 1))
@@ -459,9 +502,16 @@
         landed(handle)
     for copy in halos + fluxes:
         copy.wait_send()
-    for copies, own, arrivals in out_there + out_cross + back_home:
+    for copies, own, arrivals in out_there + back_home:
         for copy in copies:
             copy.wait_send()
+
+    @pl.when(inside)
+    def _():
+        for copies, arrivals in out_cross:
+            for copy in copies:
+                copy.wait_send()
+
     ocean_copy.wait()
     surf_copy.wait()
 
@@ -516,7 +566,7 @@
             pltpu.SMEM((FIELDS,), F32), pltpu.SMEM((FIELDS,), F32),
             vmem(2, 128), vmem(2, 128, dtype=jnp.int32), vmem(2, 128, dtype=jnp.int32),
             vmem(4, 256, dtype=jnp.int32), vmem(4, 256),
-            vmem(2, 1008, 128), vmem(13, QS, 40, 128), vmem(13, QS, 40, 128), vmem(4, 40, 128),
+            vmem(2, 1008, 128), vmem(2, DYN_STEPS, 13, QS, 40, 128), vmem(2, 4, 40, 128),
             *[vmem(8, 72, 128)] * 5, *[vmem(8, 56, 128)] * 5,
             vmem(LEV, 8, 128), vmem(LEV, 8, 128),
             vmem(320, 128),

time: 39.1 us -> 34.9 us (0.89)
  the two profiles are of different devices: /device:TPU:1 before, /device:TPU:161 now
where the time goes in v4:
time: 34.9 us; the launch traced here: 34.8 us
  Pallas kernels  34.1 us (98%)
  between operations  0.64 us (2%)
    pallas_call x1, Pallas kernels, local(): pl.pallas_call(functools.partial(kernel, n_atm, n_ocn), out_shape=(jax.Sh...  32.1 us
    pallas_call x1, Pallas kernels, local(): pl.pallas_call(finish, out_shape=(jax.ShapeDtypeStruct((1008, 128), F32),...  2 us

profile of v4, /device:TPU:161, one launch (start us, length us, event | category | flops | bytes accessed | tf_op | source)
XLA Modules:
  0.0 34.8 jit_solution(14775187087420233102)
XLA Ops:
  0.6 32.1 %shard_map.157 = (f32[8,72,128]{2,1,0:T(8,128)}, f32[8,56,128]{2,1,0:T(8,128)}, f32[320,128]{1,0:T(8,128)}, f32[2,128]{1,0:T(2,128)}) custom-call(f32[1008,128]{1,0:T(8,128)} %bitcast.28, f32[9]{0:T(128)} %ld.1, f32[9]{0:T(128)} %lw.1, f32[7]{0:T(128)} %vr.1, f32[7]{0:T(128)} %cr.1, f32[2,128]{1,0:T(2,128)} %bitcast.30, s32[2,128]{1,0:T(2,128)} %bitcast.31, ...), custom_call_target="tpu_custom_call" | custom-call | tf_op jit(solution)/shard_map/pallas_call | solution.py:554
  32.8 2.0 %shard_map.158 = (f32[1008,128]{1,0:T(8,128)}, f32[320,128]{1,0:T(8,128)}, f32[2,128]{1,0:T(2,128)}) custom-call(f32[8,72,128]{2,1,0:T(8,128)} %get-tuple-element.10.ba0, f32[8,56,128]{2,1,0:T(8,128)} %get-tuple-element.11.ba1, f32[320,128]{1,0:T(8,128)} %get-tuple-element.12.ocean, f32[2,128]{1,0:T(2,128)} %get-tuple-element.13.surf), custom_call_target="tpu_custom_call" | custom-call | tf_op jit(solution)/shard_map/pallas_call | solution.py:590

commit v5 on v4

--- a/solution.py
+++ b/solution.py
@@ -197,13 +197,10 @@
 
     def send_across(g):
         copies = [
-            remote(gives[g].at[p], adds[g].at[o], c_send.at[g, p], c_recv.at[g, o], (cross, p))
+            remote(gives[g].at[p], adds[g].at[o], c_send.at[g], c_recv.at[g], (cross, p))
             for p in others
         ]
-        arrivals = [
-            remote(gives[g].at[p], adds[g].at[p], c_send.at[g, p], c_recv.at[g, p], (cross, p))
-            for p in others
-        ]
+        whole = remote(gives[g], adds[g], c_send.at[g], c_recv.at[g], (cross, o))
 
         @pl.when(inside)
         def _():
@@ -214,7 +211,7 @@
         def _():
             adds[g][...] = jnp.zeros(adds[g].shape, F32)
 
-        return copies, arrivals
+        return whole
 
     contribute(0)
 
@@ -266,28 +263,24 @@
 
     def exchange(src, dst, send, recv, own_sem, g):
         copies = [
-            remote(src.at[p], dst.at[o], send.at[g, p], recv.at[g, o], (a, p)) for p in peers
+            remote(src.at[p], dst.at[o], send.at[g], recv.at[g], (a, p)) for p in peers
         ]
         own = pltpu.make_async_copy(src.at[o], dst.at[o], own_sem)
         for copy in copies:
             copy.start()
         own.start()
-        arrivals = [
-            remote(src.at[p], dst.at[p], send.at[g, p], recv.at[g, p], (a, p)) for p in peers
-        ]
-        return copies, own, arrivals
+        seven = pl.ds(0, n_ocn - 1)
+        return remote(src.at[seven], dst.at[seven], send.at[g], recv.at[g], (a, peers[0])), own
 
     def crossed(handle):
         @pl.when(inside)
         def _():
-            for copy in handle[1]:
-                copy.wait_recv()
+            handle.wait_recv()
 
     def landed(handle):
-        copies, own, arrivals = handle
+        whole, own = handle
         own.wait()
-        for copy in arrivals:
-            copy.wait_recv()
+        whole.wait_recv()
 
     out_there = []
     for g in range(2):
@@ -498,20 +491,20 @@
     surf_copy = pltpu.make_async_copy(sout, out_surf, out_sem.at[1])
     surf_copy.start()
 
+    for copy in halos + fluxes:
+        copy.wait_send()
+    for whole, own in out_there:
+        whole.wait_send()
+
+    @pl.when(inside)
+    def _():
+        for whole in out_cross:
+            whole.wait_send()
+
+    for whole, own in back_home:
+        whole.wait_send()
     for handle in back_home:
         landed(handle)
-    for copy in halos + fluxes:
-        copy.wait_send()
-    for copies, own, arrivals in out_there + back_home:
-        for copy in copies:
-            copy.wait_send()
-
-    @pl.when(inside)
-    def _():
-        for copies, arrivals in out_cross:
-            for copy in copies:
-                copy.wait_send()
-
     ocean_copy.wait()
     surf_copy.wait()
 
@@ -576,7 +569,7 @@
             vmem(320, 128), vmem(2, 128),
             vmem(8, 128), vmem(8, 128), vmem(8, 128),
             dma((14,)), dma((2,)), dma((2,)), dma((8,)), dma((8,)),
-            dma((2, 8)), dma((2, 8)), dma((2, 8)), dma((2, 8)), dma((2, 8)), dma((2, 8)), dma((4,)),
+            *[dma((2,))] * 6, dma((4,)),
             dma((2,)), dma((2,)), dma((2,)),
         ],
         compiler_params=pltpu.CompilerParams(

time: 34.9 us -> 34.1 us (0.977)
  Pallas kernels: 34.1 us -> 33.3 us
    pallas_call x1, Pallas kernels: 32.1 us -> 31.3 us  [local(): pl.pallas_call(functools.partial(kernel, n_atm, n_ocn), out_shape=(jax.Sh...]
where the time goes in v5:
time: 34.1 us; the launch traced here: 34 us
  Pallas kernels  33.3 us (98%)
  between operations  0.64 us (2%)
    pallas_call x1, Pallas kernels, local(): pl.pallas_call(functools.partial(kernel, n_atm, n_ocn), out_shape=(jax.Sh...  31.3 us
    pallas_call x1, Pallas kernels, local(): pl.pallas_call(finish, out_shape=(jax.ShapeDtypeStruct((1008, 128), F32),...  2 us

profile of v5, /device:TPU:161, one launch (start us, length us, event | category | flops | bytes accessed | tf_op | source)
XLA Modules:
  0.0 34.0 jit_solution(2336955936946224644)
XLA Ops:
  0.6 31.3 %shard_map.157 = (f32[8,72,128]{2,1,0:T(8,128)}, f32[8,56,128]{2,1,0:T(8,128)}, f32[320,128]{1,0:T(8,128)}, f32[2,128]{1,0:T(2,128)}) custom-call(f32[1008,128]{1,0:T(8,128)} %bitcast.28, f32[9]{0:T(128)} %ld.1, f32[9]{0:T(128)} %lw.1, f32[7]{0:T(128)} %vr.1, f32[7]{0:T(128)} %cr.1, f32[2,128]{1,0:T(2,128)} %bitcast.30, s32[2,128]{1,0:T(2,128)} %bitcast.31, ...), custom_call_target="tpu_custom_call" | custom-call | tf_op jit(solution)/shard_map/pallas_call | solution.py:547
  32.0 2.0 %shard_map.158 = (f32[1008,128]{1,0:T(8,128)}, f32[320,128]{1,0:T(8,128)}, f32[2,128]{1,0:T(2,128)}) custom-call(f32[8,72,128]{2,1,0:T(8,128)} %get-tuple-element.10.ba0, f32[8,56,128]{2,1,0:T(8,128)} %get-tuple-element.11.ba1, f32[320,128]{1,0:T(8,128)} %get-tuple-element.12.ocean, f32[2,128]{1,0:T(2,128)} %get-tuple-element.13.surf), custom_call_target="tpu_custom_call" | custom-call | tf_op jit(solution)/shard_map/pallas_call | solution.py:583

commit v6 on v5

--- a/solution.py
+++ b/solution.py
@@ -51,7 +51,7 @@
     nb, dd, coef,
     sa0, ra0, sc0, rc0, pa0, sa1, ra1, sc1, rc1, pa1,
     xa, xb,
-    oc_o, nbr_e, fsrc_e, fw_e,
+    oc_o, nbr_e, fsrc_e, fw_e, el_out, er_out, el_in, er_in,
     st, hs, mm, ff, uu, oout, sout,
     fl, fl_l, fl_r,
     local_sem, halo_send, halo_recv, oh_send, oh_recv,
@@ -237,24 +237,17 @@
             st[pl.ds(u * OROW + f * 24, OLEV), :] = piece
             st[pl.ds(u * OROW + f * 24 + OLEV, 4), :] = unused
 
-    def tiles(u):
-        return st.at[pl.ds(u * OROW, 2 * OROW)]
-
-    last, first = pl.ds(896, 128), pl.ds(0, 128)
-    low, high = pl.ds(128, 128), pl.ds(1280, 128)
-    edge = [
-        (tiles(8), tiles(0), right_id),
-        (nbr.at[:, last], nbr_e.at[:, low], right_id),
-        (fsrc.at[:, last], fsrc_e.at[:, low], right_id),
-        (fw.at[:, last], fw_e.at[:, low], right_id),
-        (tiles(2), tiles(10), left_id),
-        (nbr.at[:, first], nbr_e.at[:, high], left_id),
-        (fsrc.at[:, first], fsrc_e.at[:, high], left_id),
-        (fw.at[:, first], fw_e.at[:, high], left_id),
-    ]
+    sides = ((el_out, 8, 1152, el_in, right_id), (er_out, 2, 256, er_in, left_id))
+    for buf, u, at, _, _ in sides:
+        for k in range(4):
+            buf[pl.ds(k * OLEV, OLEV), :] = st[pl.ds(u * OROW + k * 24, OLEV), :]
+        buf[pl.ds(80, NBR), :] = nbr_e[:, pl.ds(at, 128)].astype(F32)
+        buf[pl.ds(86, NW), :] = fsrc_e[:, pl.ds(at, 128)].astype(F32)
+        buf[pl.ds(90, NW), :] = fw_e[:, pl.ds(at, 128)]
+        buf[pl.ds(94, 2), :] = jnp.zeros((2, 128), F32)
     edges = [
-        remote(src, dst, oh_send.at[i], oh_recv.at[i], device)
-        for i, (src, dst, device) in enumerate(edge)
+        remote(buf, into, oh_send.at[i], oh_recv.at[i], device)
+        for i, (buf, _, _, into, device) in enumerate(sides)
     ]
     for copy in edges:
         copy.start()
@@ -303,9 +296,14 @@
         active.append(jnp.sum(mark, axis=0, keepdims=True))
 
     for copy in edges:
-        copy.wait_recv()
-    for copy in edges:
-        copy.wait_send()
+        copy.wait()
+    for buf, u, at in ((el_in, 0, 128), (er_in, 10, 1280)):
+        for k in range(4):
+            st[pl.ds(u * OROW + k * 24, OLEV), :] = buf[pl.ds(k * OLEV, OLEV), :]
+            st[pl.ds(u * OROW + k * 24 + OLEV, 4), :] = unused
+        nbr_e[:, pl.ds(at, 128)] = buf[pl.ds(80, NBR), :].astype(jnp.int32)
+        fsrc_e[:, pl.ds(at, 128)] = buf[pl.ds(86, NW), :].astype(jnp.int32)
+        fw_e[:, pl.ds(at, 128)] = buf[pl.ds(90, NW), :]
 
     def build(u, carry):
         at = pl.multiple_of(u * 128, 128)
@@ -564,6 +562,7 @@
             vmem(LEV, 8, 128), vmem(LEV, 8, 128),
             vmem(320, 128),
             vmem(NBR, 1536, dtype=jnp.int32), vmem(NW, 1536, dtype=jnp.int32), vmem(NW, 1536),
+            *[vmem(96, 128)] * 4,
             vmem(NT * OROW, 128), vmem(NT, PARTS * OROW, 128, dtype=BF16),
             vmem(NT - 2, 384, 128, dtype=BF16), vmem(NT * OROW, 128), vmem(16, 128),
             vmem(320, 128), vmem(2, 128),

time: 34.1 us -> 33.7 us (0.988)
  Pallas kernels: 33.3 us -> 32.9 us
    pallas_call x1, Pallas kernels: 31.3 us -> 31 us  [local(): pl.pallas_call(functools.partial(kernel, n_atm, n_ocn), out_shape=(jax.Sh...]
where the time goes in v6:
time: 33.7 us; the launch traced here: 33.6 us
  Pallas kernels  32.9 us (98%)
  between operations  0.64 us (2%)
    pallas_call x1, Pallas kernels, local(): pl.pallas_call(functools.partial(kernel, n_atm, n_ocn), out_shape=(jax.Sh...  31 us
    pallas_call x1, Pallas kernels, local(): pl.pallas_call(finish, out_shape=(jax.ShapeDtypeStruct((1008, 128), F32),...  2 us

profile of v6, /device:TPU:161, one launch (start us, length us, event | category | flops | bytes accessed | tf_op | source)
XLA Modules:
  0.0 33.6 jit_solution(11706279903516045080)
XLA Ops:
  0.6 31.0 %shard_map.157 = (f32[8,72,128]{2,1,0:T(8,128)}, f32[8,56,128]{2,1,0:T(8,128)}, f32[320,128]{1,0:T(8,128)}, f32[2,128]{1,0:T(2,128)}) custom-call(f32[1008,128]{1,0:T(8,128)} %bitcast.28, f32[9]{0:T(128)} %ld.1, f32[9]{0:T(128)} %lw.1, f32[7]{0:T(128)} %vr.1, f32[7]{0:T(128)} %cr.1, f32[2,128]{1,0:T(2,128)} %bitcast.30, s32[2,128]{1,0:T(2,128)} %bitcast.31, ...), custom_call_target="tpu_custom_call" | custom-call | tf_op jit(solution)/shard_map/pallas_call | solution.py:545
  31.6 2.0 %shard_map.158 = (f32[1008,128]{1,0:T(8,128)}, f32[320,128]{1,0:T(8,128)}, f32[2,128]{1,0:T(2,128)}) custom-call(f32[8,72,128]{2,1,0:T(8,128)} %get-tuple-element.10.ba0, f32[8,56,128]{2,1,0:T(8,128)} %get-tuple-element.11.ba1, f32[320,128]{1,0:T(8,128)} %get-tuple-element.12.ocean, f32[2,128]{1,0:T(2,128)} %get-tuple-element.13.surf), custom_call_target="tpu_custom_call" | custom-call | tf_op jit(solution)/shard_map/pallas_call | solution.py:582
